TPU v7x, 512 devices: a whole 4x4x16 slice. The times are simulated.
512 devices in a mesh: ctx: 64 (over z_hi, y, x), tp: 8 (over z_lo, core).
Axes of the slice: x: 4, y: 4, z: 16 (z_hi: 4, z_lo: 4; z = z_hi * 4 + z_lo), core: 2. Of those that a mesh axis runs over, the one named last changes fastest.
Arguments:
- query_gate: bfloat16 [4096, 8192], P('tp', 'ctx'), may hold values from -6 to 6
- key_gate: bfloat16 [4096, 8192], P('tp', 'ctx'), may hold values from -6 to 6
- value_input: bfloat16 [4096, 8192], P('tp', 'ctx'), may hold values from -6 to 6
- long_filter: float32 [4096, 8192], P('tp', 'ctx'), may hold values from -1.2 to 1.2
- skip_gain: float32 [4096], P('tp'), may hold values from -4 to 4
- out_weight: bfloat16 [4096, 4096], P('tp', 'ctx'), may hold values from -0.09375 to 0.09375
- out_bias: float32 [4096], P('tp'), may hold values from -3 to 3
Outputs:
- mixed_out: bfloat16 [4096, 8192], P('tp', 'ctx')
All inputs are finite; a program needn't handle non-finite values.
Results may differ from a plain program's by a relative error of at most 0.0046.
Values may be sent and summed in bfloat16 or wider, within the bound.
A program may use at most 64 MiB of HBM per device.

v0:
```python
import math

import jax
import jax.numpy as jnp
from jax import lax
from jax.sharding import PartitionSpec as P

TWO_PI = 2.0 * math.pi


def swapped(value, axis, bit):
    mask = 2**bit
    pairs = [(source, source ^ mask) for source in range(lax.axis_size(axis))]
    return lax.ppermute(value, axis, pairs)


def unit_circle(numer, denom):
    angles = TWO_PI / denom * (numer % denom).astype(jnp.float32)
    return (jnp.cos(angles), jnp.sin(angles))


def rotate(parts, cos_part, sin_part):
    real_part, imag_part = parts
    return (
        real_part * cos_part - imag_part * sin_part,
        real_part * sin_part + imag_part * cos_part,
    )


def precise_dot(left, right):
    return jnp.dot(left, right, precision=lax.Precision.HIGHEST, preferred_element_type=jnp.float32)


def transform_last(parts, inverse):
    real_part, imag_part = parts
    full_shape = real_part.shape
    extent = full_shape[-1]
    block_width = min(extent, 128)
    flat_real = real_part.reshape(-1, extent)
    flat_imag = imag_part.reshape(-1, extent)
    row_index = lax.iota(jnp.int32, extent)
    direction = 1.0 if inverse else -1.0

    def one_block(block_index, buffers):
        col_index = block_index * block_width + lax.iota(jnp.int32, block_width)
        cos_part, sin_part = unit_circle(row_index[:, None] * col_index[None, :], extent)
        sin_part = direction * sin_part
        block_real = precise_dot(flat_real, cos_part) - precise_dot(flat_imag, sin_part)
        block_imag = precise_dot(flat_real, sin_part) + precise_dot(flat_imag, cos_part)
        return (block_real, block_imag)

    empty_buf = jnp.zeros_like(flat_real)
    out_real, out_imag = lax.fori_loop(0, extent // block_width, one_block, (empty_buf, empty_buf))
    return (out_real.reshape(full_shape), out_imag.reshape(full_shape))


def twist(signals, positions, seq_total, axis):
    cos_part, sin_part = unit_circle(positions, 2 * seq_total)
    real_part = jnp.concatenate([signals, signals * cos_part], axis)
    imag_part = jnp.concatenate([jnp.zeros_like(signals), -signals * sin_part], axis)
    return (real_part, imag_part)


def untwist(parts, positions, seq_total, axis):
    cos_part, sin_part = unit_circle(positions, 2 * seq_total)
    first_real = lax.index_in_dim(parts[0], 0, axis, keepdims=False)
    second_real = lax.index_in_dim(parts[0], 1, axis, keepdims=False)
    second_imag = lax.index_in_dim(parts[1], 1, axis, keepdims=False)
    return (first_real + cos_part * second_real - sin_part * second_imag) / (2.0 * seq_total)


def spectral_middle(parts, freq_base, seq_total, length):
    offsets = lax.iota(jnp.int32, length)
    cos_part, sin_part = unit_circle(freq_base * offsets, seq_total)
    parts = rotate(parts, cos_part, -sin_part)
    real_part, imag_part = transform_last(parts, False)
    filter_real = real_part[..., 0:1, :, :]
    filter_imag = imag_part[..., 0:1, :, :]
    signal_real = real_part[..., 1:2, :, :]
    signal_imag = imag_part[..., 1:2, :, :]
    product_real = filter_real * signal_real - filter_imag * signal_imag
    product_imag = filter_real * signal_imag + filter_imag * signal_real
    back = transform_last((product_real, product_imag), True)
    return rotate(back, cos_part, sin_part)


def section_conv(signals, members, length, seq_total):
    own_index = lax.axis_index("ctx")
    levels = members.bit_length() - 1
    positions = own_index * length + lax.iota(jnp.int32, length)
    real_part, imag_part = twist(signals[None], positions, seq_total, 0)
    for section_bit in reversed(range(levels)):
        stride = 1 << section_bit
        partner = swapped((real_part, imag_part), "ctx", section_bit)
        upper_half = own_index // stride % 2 == 1
        cos_part, sin_part = unit_circle(own_index % stride * (members // (2 * stride)), members)
        difference = rotate((partner[0] - real_part, partner[1] - imag_part), cos_part, -sin_part)
        real_part = jnp.where(upper_half, difference[0], real_part + partner[0])
        imag_part = jnp.where(upper_half, difference[1], imag_part + partner[1])
    freq_base = jnp.zeros((), jnp.int32)
    for section_bit in range(levels):
        freq_base = freq_base + own_index // (1 << section_bit) % 2 * (
            1 << levels - 1 - section_bit
        )
    spectra = spectral_middle((real_part, imag_part), freq_base, seq_total, length)
    for section_bit in range(levels):
        stride = 1 << section_bit
        partner = swapped((spectra[0], spectra[1]), "ctx", section_bit)
        upper_half = own_index // stride % 2 == 1
        cos_part, sin_part = unit_circle(own_index % stride * (members // (2 * stride)), members)
        turned_partner = rotate(partner, cos_part, sin_part)
        turned_own = rotate(spectra, cos_part, sin_part)
        spectra = (
            jnp.where(upper_half, partner[0] - turned_own[0], spectra[0] + turned_partner[0]),
            jnp.where(upper_half, partner[1] - turned_own[1], spectra[1] + turned_partner[1]),
        )
    return untwist(spectra, positions, seq_total, 0)[0]


def on_device(query_gate, key_gate, value_input, long_filter, skip_gain, out_weight, out_bias):
    members = lax.axis_size("ctx")
    channels, length = long_filter.shape
    seq_total = members * length
    full_rows = lax.all_gather(out_weight, "ctx", axis=1, tiled=True)
    products = key_gate.astype(jnp.float32) * value_input.astype(jnp.float32)
    signals = jnp.stack([long_filter, products])
    long_conv = section_conv(signals, members, length, seq_total)
    long_conv = long_conv + skip_gain[:, None] * products
    gated_values = (query_gate.astype(jnp.float32) * long_conv).astype(jnp.bfloat16)
    mixed_out = lax.psum_scatter(
        lax.dot_general(
            full_rows, gated_values, (((0,), (0,)), ((), ())), preferred_element_type=jnp.float32
        ),
        "tp",
        scatter_dimension=0,
        tiled=True,
    )
    return (mixed_out + out_bias[:, None]).astype(jnp.bfloat16)


def solution(mesh):
    placed = (
        P("tp", "ctx"),
        P("tp", "ctx"),
        P("tp", "ctx"),
        P("tp", "ctx"),
        P("tp"),
        P("tp", "ctx"),
        P("tp"),
    )
    return jax.shard_map(
        on_device, mesh=mesh, in_specs=placed, out_specs=P("tp", "ctx"), check_vma=False
    )
```

profile of v0, /device:TPU:1, one launch (start us, length us, event | category | flops | bytes accessed | tf_op | source)
XLA Modules:
  0.0 948.2 jit_solution(1130576501298431925)
XLA Ops:
  10.7 16.3 %collective-permute-start = (f32[2,2,512,128]{3,2,1,0:T(8,128)}, f32[2,2,512,128]{3,2,1,0:T(8,128)S(1)}, u32[]{:S(2)}, u32[]{:S(2)}) collective-permute-start(f32[2,2,512,128]{3,2,1,0:T(8,128)} %pad_maximum_fusion), channel_id=1, source_target_pairs={{0,256},{8,264},{16,272},{24,280},{32,288},{40,296},{48,304},{56,3... | collective-permute-start | bytes 3145736 | tf_op jit(solution)/shard_map/ppermute | solution.py:14
  30.2 32.6 %collective-permute-done = f32[2,2,512,128]{3,2,1,0:T(8,128)S(1)} collective-permute-done((f32[2,2,512,128]{3,2,1,0:T(8,128)}, f32[2,2,512,128]{3,2,1,0:T(8,128)S(1)}, u32[]{:S(2)}, u32[]{:S(2)}) %collective-permute-start) | collective-permute-done | bytes 1048608 | tf_op jit(solution)/shard_map/ppermute | solution.py:14
  63.7 42.4 %collective-permute-done.1 = f32[2,2,512,128]{3,2,1,0:T(8,128)} collective-permute-done((f32[2,2,512,128]{3,2,1,0:T(8,128)}, f32[2,2,512,128]{3,2,1,0:T(8,128)}, u32[]{:S(2)}, u32[]{:S(2)}) %collective-permute-start.1) | collective-permute-done | bytes 1048608 | tf_op jit(solution)/shard_map/ppermute | solution.py:14
  109.1 87.9 %collective-permute-start.2 = (f32[2,2,512,128]{3,2,1,0:T(8,128)}, f32[2,2,512,128]{3,2,1,0:T(8,128)S(1)}, u32[]{:S(2)}, u32[]{:S(2)}) collective-permute-start(f32[2,2,512,128]{3,2,1,0:T(8,128)} %get-tuple-element.46), channel_id=1, source_target_pairs={{0,128},{8,136},{16,144},{24,152},{32,160},{40,168},{48,176},{56,1... | collective-permute-start | bytes 3145736 | tf_op jit(solution)/shard_map/ppermute | solution.py:14
  199.2 167.2 %collective-permute-done.2 = f32[2,2,512,128]{3,2,1,0:T(8,128)S(1)} collective-permute-done((f32[2,2,512,128]{3,2,1,0:T(8,128)}, f32[2,2,512,128]{3,2,1,0:T(8,128)S(1)}, u32[]{:S(2)}, u32[]{:S(2)}) %collective-permute-start.2) | collective-permute-done | bytes 1048608 | tf_op jit(solution)/shard_map/ppermute | solution.py:14
  367.3 21.6 %collective-permute-done.3 = f32[2,2,512,128]{3,2,1,0:T(8,128)} collective-permute-done((f32[2,2,512,128]{3,2,1,0:T(8,128)S(1)}, f32[2,2,512,128]{3,2,1,0:T(8,128)}, u32[]{:S(2)}, u32[]{:S(2)}) %collective-permute-start.3) | collective-permute-done | bytes 1048608 | tf_op jit(solution)/shard_map/ppermute | solution.py:14
  392.1 4.8 collective-permute-start.4
  399.1 20.8 %collective-permute-done.4 = f32[2,2,512,128]{3,2,1,0:T(8,128)S(1)} collective-permute-done((f32[2,2,512,128]{3,2,1,0:T(8,128)}, f32[2,2,512,128]{3,2,1,0:T(8,128)S(1)}, u32[]{:S(2)}, u32[]{:S(2)}) %collective-permute-start.4) | collective-permute-done | bytes 1048608 | tf_op jit(solution)/shard_map/ppermute | solution.py:14
  421.0 21.6 %collective-permute-done.5 = f32[2,2,512,128]{3,2,1,0:T(8,128)} collective-permute-done((f32[2,2,512,128]{3,2,1,0:T(8,128)S(1)}, f32[2,2,512,128]{3,2,1,0:T(8,128)}, u32[]{:S(2)}, u32[]{:S(2)}) %collective-permute-start.5) | collective-permute-done | bytes 1048608 | tf_op jit(solution)/shard_map/ppermute | solution.py:14
  450.4 19.7 %collective-permute-done.6 = f32[2,2,512,128]{3,2,1,0:T(8,128)S(1)} collective-permute-done((f32[2,2,512,128]{3,2,1,0:T(8,128)S(1)}, f32[2,2,512,128]{3,2,1,0:T(8,128)S(1)}, u32[]{:S(2)}, u32[]{:S(2)}) %collective-permute-start.6) | collective-permute-done | bytes 1048608 | tf_op jit(solution)/shard_map/ppermute | solution.py:14
  471.0 21.6 %collective-permute-done.7 = f32[2,2,512,128]{3,2,1,0:T(8,128)} collective-permute-done((f32[2,2,512,128]{3,2,1,0:T(8,128)S(1)}, f32[2,2,512,128]{3,2,1,0:T(8,128)}, u32[]{:S(2)}, u32[]{:S(2)}) %collective-permute-start.7) | collective-permute-done | bytes 1048608 | tf_op jit(solution)/shard_map/ppermute | solution.py:14
  494.9 4.7 collective-permute-start.8
  502.0 18.8 %collective-permute-done.8 = f32[2,2,512,128]{3,2,1,0:T(8,128)S(1)} collective-permute-done((f32[2,2,512,128]{3,2,1,0:T(8,128)S(1)}, f32[2,2,512,128]{3,2,1,0:T(8,128)S(1)}, u32[]{:S(2)}, u32[]{:S(2)}) %collective-permute-start.8) | collective-permute-done | bytes 1048608 | tf_op jit(solution)/shard_map/ppermute | solution.py:14
  521.7 21.6 %collective-permute-done.9 = f32[2,2,512,128]{3,2,1,0:T(8,128)} collective-permute-done((f32[2,2,512,128]{3,2,1,0:T(8,128)S(1)}, f32[2,2,512,128]{3,2,1,0:T(8,128)}, u32[]{:S(2)}, u32[]{:S(2)}) %collective-permute-start.9) | collective-permute-done | bytes 1048608 | tf_op jit(solution)/shard_map/ppermute | solution.py:14
  551.9 17.9 %collective-permute-done.10 = f32[2,2,512,128]{3,2,1,0:T(8,128)S(1)} collective-permute-done((f32[2,2,512,128]{3,2,1,0:T(8,128)}, f32[2,2,512,128]{3,2,1,0:T(8,128)S(1)}, u32[]{:S(2)}, u32[]{:S(2)}) %collective-permute-start.10) | collective-permute-done | bytes 1048608 | tf_op jit(solution)/shard_map/ppermute | solution.py:14
  569.8 23.3 %collective-permute-done.11 = f32[2,2,512,128]{3,2,1,0:T(8,128)S(1)} collective-permute-done((f32[2,2,512,128]{3,2,1,0:T(8,128)S(1)}, f32[2,2,512,128]{3,2,1,0:T(8,128)S(1)}, u32[]{:S(2)}, u32[]{:S(2)}) %collective-permute-start.11) | collective-permute-done | bytes 1048608 | tf_op jit(solution)/shard_map/ppermute | solution.py:14
  608.7 6.0 collective-permute-done.12
  614.6 12.3 %collective-permute-done.13 = f32[2,1,512,128]{3,2,1,0:T(8,128)S(1)} collective-permute-done((f32[2,1,512,128]{3,2,1,0:T(8,128)S(1)}, f32[2,1,512,128]{3,2,1,0:T(8,128)S(1)}, u32[]{:S(2)}, u32[]{:S(2)}) %collective-permute-start.13) | collective-permute-done | bytes 524320 | tf_op jit(solution)/shard_map/ppermute | solution.py:14
  627.1 4.6 collective-permute-start.14
  633.9 7.1 collective-permute-done.14
  641.0 11.9 %collective-permute-done.15 = f32[2,1,512,128]{3,2,1,0:T(8,128)S(1)} collective-permute-done((f32[2,1,512,128]{3,2,1,0:T(8,128)S(1)}, f32[2,1,512,128]{3,2,1,0:T(8,128)S(1)}, u32[]{:S(2)}, u32[]{:S(2)}) %collective-permute-start.15) | collective-permute-done | bytes 524320 | tf_op jit(solution)/shard_map/ppermute | solution.py:14
  663.2 11.3 %collective-permute-done.17 = f32[2,1,512,128]{3,2,1,0:T(8,128)S(1)} collective-permute-done((f32[2,1,512,128]{3,2,1,0:T(8,128)S(1)}, f32[2,1,512,128]{3,2,1,0:T(8,128)S(1)}, u32[]{:S(2)}, u32[]{:S(2)}) %collective-permute-start.17) | collective-permute-done | bytes 524320 | tf_op jit(solution)/shard_map/ppermute | solution.py:14
  681.8 10.2 %collective-permute-done.18 = f32[2,1,512,128]{3,2,1,0:T(8,128)S(1)} collective-permute-done((f32[2,1,512,128]{3,2,1,0:T(8,128)S(1)}, f32[2,1,512,128]{3,2,1,0:T(8,128)S(1)}, u32[]{:S(2)}, u32[]{:S(2)}) %collective-permute-start.18) | collective-permute-done | bytes 524320 | tf_op jit(solution)/shard_map/ppermute | solution.py:14
  692.0 8.6 collective-permute-done.19
  700.8 9.2 collective-permute-start.20
  712.0 97.9 %collective-permute-done.20 = f32[2,1,512,128]{3,2,1,0:T(8,128)S(1)} collective-permute-done((f32[2,1,512,128]{3,2,1,0:T(8,128)S(1)}, f32[2,1,512,128]{3,2,1,0:T(8,128)S(1)}, u32[]{:S(2)}, u32[]{:S(2)}) %collective-permute-start.20) | collective-permute-done | bytes 524320 | tf_op jit(solution)/shard_map/ppermute | solution.py:14
  809.9 11.4 %collective-permute-done.21 = f32[2,1,512,128]{3,2,1,0:T(8,128)S(1)} collective-permute-done((f32[2,1,512,128]{3,2,1,0:T(8,128)S(1)}, f32[2,1,512,128]{3,2,1,0:T(8,128)S(1)}, u32[]{:S(2)}, u32[]{:S(2)}) %collective-permute-start.21) | collective-permute-done | bytes 524320 | tf_op jit(solution)/shard_map/ppermute | solution.py:14
  821.6 10.9 %collective-permute-start.22 = (f32[2,1,512,128]{3,2,1,0:T(8,128)S(1)}, f32[2,1,512,128]{3,2,1,0:T(8,128)S(1)}, u32[]{:S(2)}, u32[]{:S(2)}) collective-permute-start(f32[2,1,512,128]{3,2,1,0:T(8,128)S(1)} %get-tuple-element.48), channel_id=1, source_target_pairs={{0,256},{8,264},{16,272},{24,280},{32,288},{40,296},{48,304},{56,3... | collective-permute-start | bytes 1572872 | tf_op jit(solution)/shard_map/ppermute | solution.py:14
  835.6 24.4 %collective-permute-done.22 = f32[2,1,512,128]{3,2,1,0:T(8,128)S(1)} collective-permute-done((f32[2,1,512,128]{3,2,1,0:T(8,128)S(1)}, f32[2,1,512,128]{3,2,1,0:T(8,128)S(1)}, u32[]{:S(2)}, u32[]{:S(2)}) %collective-permute-start.22) | collective-permute-done | bytes 524320 | tf_op jit(solution)/shard_map/ppermute | solution.py:14
  860.0 11.3 %collective-permute-done.23 = f32[2,1,512,128]{3,2,1,0:T(8,128)S(1)} collective-permute-done((f32[2,1,512,128]{3,2,1,0:T(8,128)S(1)}, f32[2,1,512,128]{3,2,1,0:T(8,128)S(1)}, u32[]{:S(2)}, u32[]{:S(2)}) %collective-permute-start.23) | collective-permute-done | bytes 524320 | tf_op jit(solution)/shard_map/ppermute | solution.py:14
  871.5 5.2 convolution_bitcast_fusion
  876.8 62.9 %reduce-scatter.2.cloned.1.call-done = f32[512,128]{0,1:T(8,128)} async-done(((f32[4096,128]{0,1:T(8,128)}), f32[512,128]{0,1:T(8,128)}) %reduce-scatter.2.cloned.1.call-update) | async-done | bytes 262160 | tf_op jit(solution)/shard_map/reduce_scatter | solution.py:130
  (78 shorter events, 85.6 us)
Async XLA Ops:
  6.5 864.9 %all-gather.2.cloned.1.call-start = ((), (), s32[]{:S(2)}) async-start(), calls=%async_computation.1 | async-start | bytes 4259840 | tf_op jit(solution)/shard_map/all_gather | solution.py:124
  10.7 52.1 %collective-permute-start = (f32[2,2,512,128]{3,2,1,0:T(8,128)}, f32[2,2,512,128]{3,2,1,0:T(8,128)S(1)}, u32[]{:S(2)}, u32[]{:S(2)}) collective-permute-start(f32[2,2,512,128]{3,2,1,0:T(8,128)} %pad_maximum_fusion), channel_id=1, source_target_pairs={{0,256},{8,264},{16,272},{24,280},{32,288},{40,296},{48,304},{56,3... | collective-permute-start | bytes 3145736 | tf_op jit(solution)/shard_map/ppermute | solution.py:14
  28.0 78.1 %collective-permute-start.1 = (f32[2,2,512,128]{3,2,1,0:T(8,128)}, f32[2,2,512,128]{3,2,1,0:T(8,128)}, u32[]{:S(2)}, u32[]{:S(2)}) collective-permute-start(f32[2,2,512,128]{3,2,1,0:T(8,128)} %concatenate.21), channel_id=1, source_target_pairs={{0,256},{8,264},{16,272},{24,280},{32,288},{40,296},{48,304},{56,3... | collective-permute-start | bytes 3145736 | tf_op jit(solution)/shard_map/ppermute | solution.py:14
  109.1 257.2 %collective-permute-start.2 = (f32[2,2,512,128]{3,2,1,0:T(8,128)}, f32[2,2,512,128]{3,2,1,0:T(8,128)S(1)}, u32[]{:S(2)}, u32[]{:S(2)}) collective-permute-start(f32[2,2,512,128]{3,2,1,0:T(8,128)} %get-tuple-element.46), channel_id=1, source_target_pairs={{0,128},{8,136},{16,144},{24,152},{32,160},{40,168},{48,176},{56,1... | collective-permute-start | bytes 3145736 | tf_op jit(solution)/shard_map/ppermute | solution.py:14
  197.0 191.9 %collective-permute-start.3 = (f32[2,2,512,128]{3,2,1,0:T(8,128)S(1)}, f32[2,2,512,128]{3,2,1,0:T(8,128)}, u32[]{:S(2)}, u32[]{:S(2)}) collective-permute-start(f32[2,2,512,128]{3,2,1,0:T(8,128)S(1)} %get-tuple-element.45), channel_id=1, source_target_pairs={{0,128},{8,136},{16,144},{24,152},{32,160},{40,168},{48,176},{56,1... | collective-permute-start | bytes 3145736 | tf_op jit(solution)/shard_map/ppermute | solution.py:14
  392.1 27.8 %collective-permute-start.4 = (f32[2,2,512,128]{3,2,1,0:T(8,128)}, f32[2,2,512,128]{3,2,1,0:T(8,128)S(1)}, u32[]{:S(2)}, u32[]{:S(2)}) collective-permute-start(f32[2,2,512,128]{3,2,1,0:T(8,128)} %get-tuple-element.44), channel_id=1, source_target_pairs={{0,64},{8,72},{16,80},{24,88},{32,96},{40,104},{48,112},{56,120},{... | collective-permute-start | bytes 3145736 | tf_op jit(solution)/shard_map/ppermute | solution.py:14
  397.0 45.6 %collective-permute-start.5 = (f32[2,2,512,128]{3,2,1,0:T(8,128)S(1)}, f32[2,2,512,128]{3,2,1,0:T(8,128)}, u32[]{:S(2)}, u32[]{:S(2)}) collective-permute-start(f32[2,2,512,128]{3,2,1,0:T(8,128)S(1)} %get-tuple-element.43), channel_id=1, source_target_pairs={{0,64},{8,72},{16,80},{24,88},{32,96},{40,104},{48,112},{56,120},{... | collective-permute-start | bytes 3145736 | tf_op jit(solution)/shard_map/ppermute | solution.py:14
  444.9 25.2 %copy-start = (f32[2,2,512,128]{3,2,1,0:T(8,128)}, f32[2,2,512,128]{3,2,1,0:T(8,128)S(1)}, u32[]{:S(2)}) copy-start(f32[2,2,512,128]{3,2,1,0:T(8,128)S(1)} %get-tuple-element.42) | copy-start | bytes 3145732
  444.9 25.2 %collective-permute-start.6 = (f32[2,2,512,128]{3,2,1,0:T(8,128)S(1)}, f32[2,2,512,128]{3,2,1,0:T(8,128)S(1)}, u32[]{:S(2)}, u32[]{:S(2)}) collective-permute-start(f32[2,2,512,128]{3,2,1,0:T(8,128)S(1)} %get-tuple-element.42), channel_id=1, source_target_pairs={{0,32},{8,40},{16,48},{24,56},{32,0},{40,8},{48,16},{56,24},{64,96... | collective-permute-start | bytes 3145736 | tf_op jit(solution)/shard_map/ppermute | solution.py:14
  448.1 44.6 %collective-permute-start.7 = (f32[2,2,512,128]{3,2,1,0:T(8,128)S(1)}, f32[2,2,512,128]{3,2,1,0:T(8,128)}, u32[]{:S(2)}, u32[]{:S(2)}) collective-permute-start(f32[2,2,512,128]{3,2,1,0:T(8,128)S(1)} %get-tuple-element.34), channel_id=1, source_target_pairs={{0,32},{8,40},{16,48},{24,56},{32,0},{40,8},{48,16},{56,24},{64,96... | collective-permute-start | bytes 3145736 | tf_op jit(solution)/shard_map/ppermute | solution.py:14
  494.9 25.8 %collective-permute-start.8 = (f32[2,2,512,128]{3,2,1,0:T(8,128)S(1)}, f32[2,2,512,128]{3,2,1,0:T(8,128)S(1)}, u32[]{:S(2)}, u32[]{:S(2)}) collective-permute-start(f32[2,2,512,128]{3,2,1,0:T(8,128)S(1)} %get-tuple-element.33), channel_id=1, source_target_pairs={{0,16},{8,24},{16,0},{24,8},{32,48},{40,56},{48,32},{56,40},{64,80... | collective-permute-start | bytes 3145736 | tf_op jit(solution)/shard_map/ppermute | solution.py:14
  499.6 43.7 %collective-permute-start.9 = (f32[2,2,512,128]{3,2,1,0:T(8,128)S(1)}, f32[2,2,512,128]{3,2,1,0:T(8,128)}, u32[]{:S(2)}, u32[]{:S(2)}) collective-permute-start(f32[2,2,512,128]{3,2,1,0:T(8,128)S(1)} %get-tuple-element.32), channel_id=1, source_target_pairs={{0,16},{8,24},{16,0},{24,8},{32,48},{40,56},{48,32},{56,40},{64,80... | collective-permute-start | bytes 3145736 | tf_op jit(solution)/shard_map/ppermute | solution.py:14
  546.3 23.6 %collective-permute-start.10 = (f32[2,2,512,128]{3,2,1,0:T(8,128)}, f32[2,2,512,128]{3,2,1,0:T(8,128)S(1)}, u32[]{:S(2)}, u32[]{:S(2)}) collective-permute-start(f32[2,2,512,128]{3,2,1,0:T(8,128)} %get-tuple-element.31), channel_id=1, source_target_pairs={{0,8},{8,0},{16,24},{24,16},{32,40},{40,32},{48,56},{56,48},{64,72... | collective-permute-start | bytes 3145736 | tf_op jit(solution)/shard_map/ppermute | solution.py:14
  549.4 43.7 %collective-permute-start.11 = (f32[2,2,512,128]{3,2,1,0:T(8,128)S(1)}, f32[2,2,512,128]{3,2,1,0:T(8,128)S(1)}, u32[]{:S(2)}, u32[]{:S(2)}) collective-permute-start(f32[2,2,512,128]{3,2,1,0:T(8,128)S(1)} %get-tuple-element.30), channel_id=1, source_target_pairs={{0,8},{8,0},{16,24},{24,16},{32,40},{40,32},{48,56},{56,48},{64,72... | collective-permute-start | bytes 3145736 | tf_op jit(solution)/shard_map/ppermute | solution.py:14
  551.6 388.1 %reduce-scatter.2.cloned.1.call-start = ((), (), s32[]{:S(2)}) async-start(), calls=%async_computation.2 | async-start | bytes 2359296 | tf_op jit(solution)/shard_map/reduce_scatter | solution.py:130
  603.4 11.3 %collective-permute-start.12 = (f32[2,1,512,128]{3,2,1,0:T(8,128)S(1)}, f32[2,1,512,128]{3,2,1,0:T(8,128)S(1)}, u32[]{:S(2)}, u32[]{:S(2)}) collective-permute-start(f32[2,1,512,128]{3,2,1,0:T(8,128)S(1)} %get-tuple-element.69), channel_id=1, source_target_pairs={{0,8},{8,0},{16,24},{24,16},{32,40},{40,32},{48,56},{56,48},{64,72... | collective-permute-start | bytes 1572872 | tf_op jit(solution)/shard_map/ppermute | solution.py:14
  606.5 20.4 %collective-permute-start.13 = (f32[2,1,512,128]{3,2,1,0:T(8,128)S(1)}, f32[2,1,512,128]{3,2,1,0:T(8,128)S(1)}, u32[]{:S(2)}, u32[]{:S(2)}) collective-permute-start(f32[2,1,512,128]{3,2,1,0:T(8,128)S(1)} %get-tuple-element.68), channel_id=1, source_target_pairs={{0,8},{8,0},{16,24},{24,16},{32,40},{40,32},{48,56},{56,48},{64,72... | collective-permute-start | bytes 1572872 | tf_op jit(solution)/shard_map/ppermute | solution.py:14
  627.1 13.9 %collective-permute-start.14 = (f32[2,1,512,128]{3,2,1,0:T(8,128)S(1)}, f32[2,1,512,128]{3,2,1,0:T(8,128)S(1)}, u32[]{:S(2)}, u32[]{:S(2)}) collective-permute-start(f32[2,1,512,128]{3,2,1,0:T(8,128)S(1)} %get-tuple-element.65), channel_id=1, source_target_pairs={{0,16},{8,24},{16,0},{24,8},{32,48},{40,56},{48,32},{56,40},{64,80... | collective-permute-start | bytes 1572872 | tf_op jit(solution)/shard_map/ppermute | solution.py:14
  631.8 21.2 %collective-permute-start.15 = (f32[2,1,512,128]{3,2,1,0:T(8,128)S(1)}, f32[2,1,512,128]{3,2,1,0:T(8,128)S(1)}, u32[]{:S(2)}, u32[]{:S(2)}) collective-permute-start(f32[2,1,512,128]{3,2,1,0:T(8,128)S(1)} %get-tuple-element.64), channel_id=1, source_target_pairs={{0,16},{8,24},{16,0},{24,8},{32,48},{40,56},{48,32},{56,40},{64,80... | collective-permute-start | bytes 1572872 | tf_op jit(solution)/shard_map/ppermute | solution.py:14
  653.3 9.9 %collective-permute-start.16 = (f32[2,1,512,128]{3,2,1,0:T(8,128)S(1)}, f32[2,1,512,128]{3,2,1,0:T(8,128)S(1)}, u32[]{:S(2)}, u32[]{:S(2)}) collective-permute-start(f32[2,1,512,128]{3,2,1,0:T(8,128)S(1)} %get-tuple-element.63), channel_id=1, source_target_pairs={{0,32},{8,40},{16,48},{24,56},{32,0},{40,8},{48,16},{56,24},{64,96... | collective-permute-start | bytes 1572872 | tf_op jit(solution)/shard_map/ppermute | solution.py:14
  656.4 18.1 %collective-permute-start.17 = (f32[2,1,512,128]{3,2,1,0:T(8,128)S(1)}, f32[2,1,512,128]{3,2,1,0:T(8,128)S(1)}, u32[]{:S(2)}, u32[]{:S(2)}) collective-permute-start(f32[2,1,512,128]{3,2,1,0:T(8,128)S(1)} %get-tuple-element.62), channel_id=1, source_target_pairs={{0,32},{8,40},{16,48},{24,56},{32,0},{40,8},{48,16},{56,24},{64,96... | collective-permute-start | bytes 1572872 | tf_op jit(solution)/shard_map/ppermute | solution.py:14
  674.8 17.1 %collective-permute-start.18 = (f32[2,1,512,128]{3,2,1,0:T(8,128)S(1)}, f32[2,1,512,128]{3,2,1,0:T(8,128)S(1)}, u32[]{:S(2)}, u32[]{:S(2)}) collective-permute-start(f32[2,1,512,128]{3,2,1,0:T(8,128)S(1)} %get-tuple-element.61), channel_id=1, source_target_pairs={{0,64},{8,72},{16,80},{24,88},{32,96},{40,104},{48,112},{56,120},{... | collective-permute-start | bytes 1572872 | tf_op jit(solution)/shard_map/ppermute | solution.py:14
  679.3 192.2 %copy-start.6 = (bf16[512,128]{1,0:T(8,128)(2,1)S(1)}, bf16[512,128]{1,0:T(8,128)(2,1)}, u32[]{:S(2)}) copy-start(bf16[512,128]{1,0:T(8,128)(2,1)} %param.9) | copy-start | bytes 393220
  679.3 192.2 %copy-start.7 = (bf16[512,128]{1,0:T(8,128)(2,1)S(1)}, bf16[512,128]{1,0:T(8,128)(2,1)}, u32[]{:S(2)}) copy-start(bf16[512,128]{1,0:T(8,128)(2,1)} %param.8) | copy-start | bytes 393220
  679.3 192.2 %copy-start.8 = (bf16[512,128]{1,0:T(8,128)(2,1)S(1)}, bf16[512,128]{1,0:T(8,128)(2,1)}, u32[]{:S(2)}) copy-start(bf16[512,128]{1,0:T(8,128)(2,1)} %param.7) | copy-start | bytes 393220
  679.3 192.2 %copy-start.9 = (f32[512]{0:T(512)S(1)}, f32[512]{0:T(512)}, u32[]{:S(2)}) copy-start(f32[512]{0:T(512)} %param.11) | copy-start | bytes 6148
  679.3 21.2 %collective-permute-start.19 = (f32[2,1,512,128]{3,2,1,0:T(8,128)S(1)}, f32[2,1,512,128]{3,2,1,0:T(8,128)S(1)}, u32[]{:S(2)}, u32[]{:S(2)}) collective-permute-start(f32[2,1,512,128]{3,2,1,0:T(8,128)S(1)} %get-tuple-element.60), channel_id=1, source_target_pairs={{0,64},{8,72},{16,80},{24,88},{32,96},{40,104},{48,112},{56,120},{... | collective-permute-start | bytes 1572872 | tf_op jit(solution)/shard_map/ppermute | solution.py:14
  700.8 109.1 %collective-permute-start.20 = (f32[2,1,512,128]{3,2,1,0:T(8,128)S(1)}, f32[2,1,512,128]{3,2,1,0:T(8,128)S(1)}, u32[]{:S(2)}, u32[]{:S(2)}) collective-permute-start(f32[2,1,512,128]{3,2,1,0:T(8,128)S(1)} %get-tuple-element.58), channel_id=1, source_target_pairs={{0,128},{8,136},{16,144},{24,152},{32,160},{40,168},{48,176},{56,1... | collective-permute-start | bytes 1572872 | tf_op jit(solution)/shard_map/ppermute | solution.py:14
  710.1 111.2 %collective-permute-start.21 = (f32[2,1,512,128]{3,2,1,0:T(8,128)S(1)}, f32[2,1,512,128]{3,2,1,0:T(8,128)S(1)}, u32[]{:S(2)}, u32[]{:S(2)}) collective-permute-start(f32[2,1,512,128]{3,2,1,0:T(8,128)S(1)} %get-tuple-element.56), channel_id=1, source_target_pairs={{0,128},{8,136},{16,144},{24,152},{32,160},{40,168},{48,176},{56,1... | collective-permute-start | bytes 1572872 | tf_op jit(solution)/shard_map/ppermute | solution.py:14
  821.6 38.4 %collective-permute-start.22 = (f32[2,1,512,128]{3,2,1,0:T(8,128)S(1)}, f32[2,1,512,128]{3,2,1,0:T(8,128)S(1)}, u32[]{:S(2)}, u32[]{:S(2)}) collective-permute-start(f32[2,1,512,128]{3,2,1,0:T(8,128)S(1)} %get-tuple-element.48), channel_id=1, source_target_pairs={{0,256},{8,264},{16,272},{24,280},{32,288},{40,296},{48,304},{56,3... | collective-permute-start | bytes 1572872 | tf_op jit(solution)/shard_map/ppermute | solution.py:14
  832.5 38.8 %collective-permute-start.23 = (f32[2,1,512,128]{3,2,1,0:T(8,128)S(1)}, f32[2,1,512,128]{3,2,1,0:T(8,128)S(1)}, u32[]{:S(2)}, u32[]{:S(2)}) collective-permute-start(f32[2,1,512,128]{3,2,1,0:T(8,128)S(1)} %get-tuple-element.47), channel_id=1, source_target_pairs={{0,256},{8,264},{16,272},{24,280},{32,288},{40,296},{48,304},{56,3... | collective-permute-start | bytes 1572872 | tf_op jit(solution)/shard_map/ppermute | solution.py:14
  871.4 68.2 %copy-start.10 = (f32[512]{0:T(512)S(1)}, f32[512]{0:T(512)}, u32[]{:S(2)}) copy-start(f32[512]{0:T(512)} %param.13) | copy-start | bytes 6148
  (5 other events, 4.9 us)
Sparse Core Ops, SparseCore 0:
  551.7 230.4 all-gather.1
  876.9 62.7 reduce-scatter.1
where the time goes:
time: 951 us; the launch traced here: 948 us
  waiting for transfers between devices  709 us (75%)
  starting transfers between devices  182 us (19%)
  other arithmetic  22.6 us (2%)
  between operations  14.9 us (2%)
  matrix products  13.3 us (1%)
    ppermute x24, waiting for transfers between devices, swapped(): return lax.ppermute(value, axis, pairs)  646 us
    ppermute x24, starting transfers between devices, swapped(): return lax.ppermute(value, axis, pairs)  181 us
    reduce_scatter x1, waiting for transfers between devices, on_device(): lax.psum_scatter(lax.dot_general(full_rows, gated_values, (((0,), (0,)),...  62.9 us
  transfers between devices with their start and end apart: 26, of which 25 were waited for; matrix products, arithmetic and copies ran while one was open for 1% of the time, Pallas kernels for 0%

commit v1 on v0

v1 whole, which is shorter than its diff:
```python
import functools

import jax
import jax.numpy as jnp
import numpy as np
from jax import lax
from jax.experimental import pallas as pl
from jax.experimental.pallas import tpu as pltpu
from jax.sharding import PartitionSpec as P

F32 = jnp.float32
BF16 = jnp.bfloat16
MESH = pl.DeviceIdType.MESH
LANES = 128
GROUP = 8


def split_bf16(array):
    high = array.astype(BF16)
    low = (array - np.asarray(high, np.float64)).astype(BF16)
    return np.asarray(high), np.asarray(low)


def transform_tables(blocks):
    n1 = np.arange(blocks)[:, None]
    k1 = np.arange(blocks)[None, :] + 0.5
    outer = 2.0 * np.pi * n1 * k1 / (2 * blocks)
    first = np.concatenate([np.cos(outer).T, -np.sin(outer).T], 0)
    first_hi, first_lo = split_bf16(first)
    scale = 2.0 / (2 * blocks * LANES)
    last = np.concatenate([np.cos(outer), -np.sin(outer)], 1) * scale
    last_hi, last_lo = split_bf16(last)
    lane = np.arange(LANES)
    inner = 2.0 * np.pi * (lane[:, None] * lane[None, :] % LANES) / LANES
    cos_part, sin_part = np.cos(inner), -np.sin(inner)
    forward = np.block([[cos_part, sin_part], [-sin_part, cos_part]])
    backward = np.block([[cos_part, -sin_part], [sin_part, cos_part]])
    turn = 2.0 * np.pi * k1.T * lane[None, :] / (2 * blocks * LANES)
    return (
        np.concatenate([first_hi, first_lo], 1),
        np.stack(split_bf16(forward)),
        np.stack(split_bf16(backward)),
        np.concatenate([last_hi, last_lo, last_hi], 1),
        np.stack([np.cos(turn), -np.sin(turn)]).astype(np.float32),
    )


def dot(left, right):
    return jnp.dot(left, right, preferred_element_type=F32)


def halves(value):
    high = value.astype(BF16)
    return high, (value - high.astype(F32)).astype(BF16)


def dot_split(value, table_ref):
    high, low = halves(value)
    return dot(high, table_ref[0]) + dot(low, table_ref[0]) + dot(high, table_ref[1])


def column(row, targets):
    lanes = lax.broadcasted_iota(jnp.int32, (targets.shape[0], row.shape[1]), 1)
    return jnp.sum(jnp.where(lanes == targets, row, 0.0), axis=1, keepdims=True)


def kernel(
    dims,
    q_ref,
    k_ref,
    v_ref,
    h_ref,
    skip_ref,
    w_ref,
    bias_ref,
    first_ref,
    fwd_ref,
    bwd_ref,
    last_ref,
    turn_ref,
    out_ref,
    cut,
    rows_in,
    query_in,
    seq_in,
    wide,
    conv_out,
    conv_wide,
    conv_in,
    gated,
    weights,
    pair_out,
    pair_in,
    own_sum,
    line_out,
    line_in,
    final,
    x_send,
    x_recv,
    q_send,
    q_recv,
    m_send,
    m_recv,
    wz_send,
    wz_recv,
    wy_send,
    wy_recv,
    r_send,
    r_recv,
    g_send,
    g_recv,
    c_send,
    c_recv,
    l_send,
    l_recv,
    e_send,
    e_recv,
):
    zh_n, y_n, x_n, zl_n = dims
    m_n = zh_n * y_n
    blocks = m_n * x_n
    me = lax.axis_index("ctx")
    tp = lax.axis_index("tp")
    x = me % x_n
    m = me // x_n
    y = m % y_n
    zh = m // y_n
    core = tp % 2
    zl = tp // 2
    channels = k_ref.shape[0]
    share = channels // x_n
    per_tp = m_n // (2 * zl_n)
    width = w_ref.shape[1]

    def at_x(step):
        return {"ctx": m * x_n + (x + step) % x_n, "tp": tp}

    def at_m(step):
        return {"ctx": (m + step) % m_n * x_n + x, "tp": tp}

    def at_zh(step):
        return {"ctx": ((zh + step) % zh_n * y_n + y) * x_n + x, "tp": tp}

    def at_y(step):
        return {"ctx": (zh * y_n + (y + step) % y_n) * x_n + x, "tp": tp}

    def at_zl(step):
        return {"ctx": me, "tp": (zl + step) % zl_n * 2 + core}

    other_core = {"ctx": me, "tp": zl * 2 + 1 - core}

    def remote(src, dst, send, recv, device):
        return pltpu.make_async_remote_copy(
            src_ref=src, dst_ref=dst, send_sem=send, recv_sem=recv, device_id=device, device_id_type=MESH
        )

    barrier = pltpu.get_barrier_semaphore()

    def greet(device):
        pl.semaphore_signal(barrier, inc=1, device_id=device, device_id_type=MESH)

    for step in range(1, x_n):
        greet(at_x(step))
    for step in range(1, m_n):
        greet(at_m(step))
    for step in range(1, zl_n):
        greet(at_zl(step))
    greet(other_core)

    products = k_ref[...].astype(F32) * v_ref[...].astype(F32)
    pieces = jnp.concatenate(
        [products.reshape(blocks, GROUP, LANES), h_ref[...].reshape(blocks, GROUP, LANES)], 1
    ).astype(BF16)
    cut[...] = pieces.reshape(x_n, m_n, 2 * GROUP, LANES)
    weights[m] = jnp.transpose(w_ref[...].astype(F32)).astype(BF16)
    own_rows = pl.ds(pl.multiple_of(x * share, share), share)
    index = lax.broadcasted_iota(jnp.int32, (share, 1), 0)
    skip = column(skip_ref[...], x * share + index)
    index = lax.broadcasted_iota(jnp.int32, (per_tp * width, 1), 0)
    bias = column(bias_ref[...], (index // width * x_n + x) * width + index % width)

    pl.semaphore_wait(barrier, (x_n - 1) + (m_n - 1) + (zl_n - 1) + 1)

    x_copies = []
    for step in range(1, x_n):
        copy = remote(
            cut.at[(x + step) % x_n], rows_in.at[:, x], x_send.at[step], x_recv.at[step], at_x(step)
        )
        copy.start()
        x_copies.append(copy)
    rows_in[:, pl.ds(x, 1)] = cut[pl.ds(x, 1)].reshape(m_n, 1, 2 * GROUP, LANES)
    query_in[pl.ds(x, 1)] = q_ref[own_rows, :][None]
    for copy in x_copies:
        copy.wait_recv()

    m_copies = []
    for step in range(1, m_n):
        copy = remote(
            rows_in.at[(m + step) % m_n], seq_in.at[m], m_send.at[step], m_recv.at[step], at_m(step)
        )
        copy.start()
        m_copies.append(copy)
    seq_in[m] = rows_in[m]
    q_copies = []
    for step in range(1, x_n):
        rows = pl.ds(pl.multiple_of((x + step) % x_n * share, share), share)
        copy = remote(q_ref.at[rows], query_in.at[x], q_send.at[step], q_recv.at[step], at_x(step))
        copy.start()
        q_copies.append(copy)
    wz_copies = []
    for step in range(1, zh_n):
        copy = remote(weights.at[m], weights.at[m], wz_send.at[step], wz_recv.at[step], at_zh(step))
        copy.start()
        wz_copies.append(copy)
    for copy in m_copies:
        copy.wait_recv()

    wide[...] = seq_in[...].reshape(blocks * 2 * GROUP, LANES).astype(F32)
    turn_re = turn_ref[0]
    turn_im = turn_ref[1]
    turn_re2 = jnp.concatenate([turn_re, turn_re], 1)
    turn_im2 = jnp.concatenate([turn_im, turn_im], 1)
    for channel in range(GROUP):
        signal = wide[pl.ds(channel, blocks, stride=2 * GROUP), :].astype(BF16)
        taps = wide[pl.ds(GROUP + channel, blocks, stride=2 * GROUP), :].astype(BF16)
        both = jnp.concatenate([signal, taps], 1)
        spread = dot(first_ref[...], jnp.concatenate([both, both], 0))
        re, im = spread[:blocks], spread[blocks:]
        turned_re = re * turn_re2 - im * turn_im2
        turned_im = re * turn_im2 + im * turn_re2
        stacked = jnp.concatenate(
            [
                jnp.concatenate([turned_re[:, :LANES], turned_im[:, :LANES]], 1),
                jnp.concatenate([turned_re[:, LANES:], turned_im[:, LANES:]], 1),
            ],
            0,
        )
        spectra = dot_split(stacked, fwd_ref)
        s_re, s_im = spectra[:blocks, :LANES], spectra[:blocks, LANES:]
        t_re, t_im = spectra[blocks:, :LANES], spectra[blocks:, LANES:]
        mixed = jnp.concatenate([s_re * t_re - s_im * t_im, s_re * t_im + s_im * t_re], 1)
        back = dot_split(mixed, bwd_ref)
        b_re, b_im = back[:, :LANES], back[:, LANES:]
        unturned = jnp.concatenate([b_re * turn_re + b_im * turn_im, b_im * turn_re - b_re * turn_im], 0)
        high, low = halves(unturned)
        conv_wide[pl.ds(channel, blocks, stride=GROUP), :] = dot(
            last_ref[...], jnp.concatenate([high, high, low], 0)
        )
    conv_out[...] = conv_wide[...].astype(BF16).reshape(m_n, x_n * GROUP, LANES)

    r_copies = []
    for step in range(1, m_n):
        copy = remote(
            conv_out.at[(m + step) % m_n], conv_in.at[m], r_send.at[step], r_recv.at[step], at_m(step)
        )
        copy.start()
        r_copies.append(copy)
    conv_in[m] = conv_out[m]
    for copy in wz_copies:
        copy.wait_recv()
    wy_copies = []
    for step in range(1, y_n):
        for part in range(zh_n):
            block = part * y_n + y
            copy = remote(
                weights.at[block],
                weights.at[block],
                wy_send.at[step, part],
                wy_recv.at[step, part],
                at_y(step),
            )
            copy.start()
            wy_copies.append(copy)
    for copy in q_copies:
        copy.wait_recv()
    for copy in r_copies:
        copy.wait_recv()

    conv = conv_in[...].astype(F32).reshape(m_n, x_n, GROUP, LANES)
    rows = rows_in[...].astype(F32)[:, :, :GROUP]
    for part in range(x_n):
        long_conv = conv[:, part].reshape(share, LANES) + skip * rows[:, part].reshape(share, LANES)
        gated[own_rows, part * LANES : (part + 1) * LANES] = (
            query_in[part].astype(F32) * long_conv
        ).astype(BF16)

    g_copies = []
    for step in range(1, x_n):
        copy = remote(gated.at[own_rows], gated.at[own_rows], g_send.at[step], g_recv.at[step], at_x(step))
        copy.start()
        g_copies.append(copy)
    for copy in wy_copies:
        copy.wait_recv()
    for copy in g_copies:
        copy.wait_recv()

    def project(target):
        block = weights[pl.ds(target * per_tp, per_tp)].reshape(per_tp * width, channels)
        return dot(block, gated[...])

    c_copies = []
    for step in range(zl_n):
        line = (zl + step + 1) % zl_n
        pair_out[step] = project(line * 2 + 1 - core)
        copy = remote(pair_out.at[step], pair_in.at[step], c_send.at[step], c_recv.at[step], other_core)
        copy.start()
        c_copies.append(copy)
    for step in range(zl_n):
        own_sum[step] = project((zl + step + 1) % zl_n * 2 + core)
    l_copies = []
    for step in range(1, zl_n):
        c_copies[step - 1].wait_recv()
        line_out[step] = (own_sum[step - 1] + pair_in[step - 1]).astype(BF16)
        copy = remote(line_out.at[step], line_in.at[step], l_send.at[step], l_recv.at[step], at_zl(step))
        copy.start()
        l_copies.append(copy)
    c_copies[zl_n - 1].wait_recv()
    total = own_sum[zl_n - 1] + pair_in[zl_n - 1] + bias
    for step in range(1, zl_n):
        l_copies[step - 1].wait_recv()
        total = total + line_in[step].astype(F32)
    total = total.astype(BF16)
    for part in range(x_n):
        final[part] = total[:, part * LANES : (part + 1) * LANES].reshape(per_tp, width, LANES)
    e_copies = []
    for step in range(1, x_n):
        copy = remote(
            final.at[(x + step) % x_n], out_ref.at[:, x], e_send.at[step], e_recv.at[step], at_x(step)
        )
        copy.start()
        e_copies.append(copy)
    out_ref[:, pl.ds(x, 1)] = final[pl.ds(x, 1)].reshape(per_tp, 1, width, LANES)
    for copy in e_copies:
        copy.wait_recv()
    for copies in (x_copies, m_copies, q_copies, wz_copies, r_copies, wy_copies, g_copies, c_copies, l_copies):
        for copy in copies:
            copy.wait_send()
    for copy in e_copies:
        copy.wait_send()


def on_device(dims, query_gate, key_gate, value_input, long_filter, skip_gain, out_weight, out_bias):
    zh_n, y_n, x_n, zl_n = dims
    m_n = zh_n * y_n
    blocks = m_n * x_n
    channels, length = key_gate.shape
    width = out_weight.shape[1]
    share = channels // x_n
    per_tp = m_n // (2 * zl_n)
    tables = [jnp.asarray(table) for table in transform_tables(blocks)]
    block_rows = per_tp * width
    span = x_n * LANES
    dma = pltpu.SemaphoreType.DMA
    out = pl.pallas_call(
        functools.partial(kernel, dims),
        out_shape=jax.ShapeDtypeStruct((per_tp, x_n, width, LANES), BF16),
        in_specs=[pl.BlockSpec(memory_space=pltpu.VMEM)] * 12,
        out_specs=pl.BlockSpec(memory_space=pltpu.VMEM),
        scratch_shapes=[
            pltpu.VMEM((x_n, m_n, 2 * GROUP, LANES), BF16),
            pltpu.VMEM((m_n, x_n, 2 * GROUP, LANES), BF16),
            pltpu.VMEM((x_n, share, LANES), BF16),
            pltpu.VMEM((m_n, x_n, 2 * GROUP, LANES), BF16),
            pltpu.VMEM((blocks * 2 * GROUP, LANES), F32),
            pltpu.VMEM((m_n, x_n * GROUP, LANES), BF16),
            pltpu.VMEM((blocks * GROUP, LANES), F32),
            pltpu.VMEM((m_n, x_n * GROUP, LANES), BF16),
            pltpu.VMEM((channels, span), BF16),
            pltpu.VMEM((m_n, width, channels), BF16),
            pltpu.VMEM((zl_n, block_rows, span), F32),
            pltpu.VMEM((zl_n, block_rows, span), F32),
            pltpu.VMEM((zl_n, block_rows, span), F32),
            pltpu.VMEM((zl_n, block_rows, span), BF16),
            pltpu.VMEM((zl_n, block_rows, span), BF16),
            pltpu.VMEM((x_n, per_tp, width, LANES), BF16),
            dma((x_n,)),
            dma((x_n,)),
            dma((x_n,)),
            dma((x_n,)),
            dma((m_n,)),
            dma((m_n,)),
            dma((zh_n,)),
            dma((zh_n,)),
            dma((y_n, zh_n)),
            dma((y_n, zh_n)),
            dma((m_n,)),
            dma((m_n,)),
            dma((x_n,)),
            dma((x_n,)),
            dma((zl_n,)),
            dma((zl_n,)),
            dma((zl_n,)),
            dma((zl_n,)),
            dma((x_n,)),
            dma((x_n,)),
        ],
        compiler_params=pltpu.CompilerParams(
            collective_id=0, has_side_effects=True, vmem_limit_bytes=48 * 1024 * 1024
        ),
        name="hyena_mixer",
    )(
        query_gate,
        key_gate,
        value_input,
        long_filter,
        skip_gain.reshape(1, channels),
        out_weight,
        out_bias.reshape(1, -1),
        *tables,
    )
    return out.reshape(per_tp * x_n * width, LANES)


def solution(mesh, dims=(4, 4, 4, 4)):
    placed = (
        P("tp", "ctx"),
        P("tp", "ctx"),
        P("tp", "ctx"),
        P("tp", "ctx"),
        P("tp"),
        P("tp", "ctx"),
        P("tp"),
    )
    return jax.shard_map(
        functools.partial(on_device, dims),
        mesh=mesh,
        in_specs=placed,
        out_specs=P("tp", "ctx"),
        check_vma=False,
    )
```

time: 951 us -> 90.7 us (0.10)
  waiting for transfers between devices: 709 us -> 0 us
  starting transfers between devices: 182 us -> 0 us
  Pallas kernels: 0 us -> 80.5 us
  other arithmetic: 22.6 us -> 0 us
  between operations: 14.9 us -> 0.06 us
  matrix products: 13.3 us -> 0 us
    ppermute x24 -> x0, waiting for transfers between devices: 646 us -> none  [swapped(): return lax.ppermute(value, axis, pairs)]
    ppermute x24 -> x0, starting transfers between devices: 181 us -> none  [swapped(): return lax.ppermute(value, axis, pairs)]
    pallas_call x0 -> x1, Pallas kernels: none -> 80.5 us  [on_device(): pl.pallas_call(functools.partial(kernel, dims), out_shape=jax.ShapeDtypeS...]
    reduce_scatter x1 -> x0, waiting for transfers between devices: 62.9 us -> none  [on_device(): lax.psum_scatter(lax.dot_general(full_rows, gated_values, (((0,), (0,)),...]
    select_n x11 -> x0, other arithmetic: 15.4 us -> none  [the longest x5 13.8 us: section_conv(): imag_part = jnp.where(upper_half, difference[1], imag_part + partner[1])]
    dot_general x9 -> x0, matrix products: 13.3 us -> none  [the longest x8 8.14 us: precise_dot(): jnp.dot(left, right, precision=lax.Precision.HIGHEST, preferred_element_t...]
  transfers between devices with their start and end apart: 26 -> 0, of which waited for: 25 -> 0; matrix products, arithmetic and copies ran while one was open for 1% -> 0% of each run, Pallas kernels for 0% -> 0%
where the time goes in v1:
time: 90.7 us; the launch traced here: 89.2 us
  Pallas kernels  80.5 us (89%)
  local copies, waits for them, and re-layouts  8.55 us (9%)
    pallas_call x1, Pallas kernels, on_device(): pl.pallas_call(functools.partial(kernel, dims), out_shape=jax.ShapeDtypeS...  80.5 us
    unnamed x24, local copies, waits for them, and re-layouts  8.55 us

profile of v1, /device:TPU:1, one launch (start us, length us, event | category | flops | bytes accessed | tf_op | source)
XLA Modules:
  0.0 89.2 jit_solution(3733451320389738367)
XLA Ops:
  0.0 0.0 copy-start.3
  0.0 0.0 copy-start.6
  0.0 0.0 copy-start.9
  0.0 1.0 %copy.13.w_ref = bf16[512,64]{1,0:T(8,128)(2,1)S(1)} copy(bf16[512,64]{0,1:T(8,128)(2,1)} %param.17) | data formatting | bytes 131072 | tf_op args[5]
  1.0 0.0 copy-done.3
  1.0 0.0 copy-done.6
  1.0 0.0 copy-done.9
  1.0 0.0 copy-start
  1.1 0.9 %copy-done = f32[512,128]{1,0:T(8,128)S(1)} copy-done((f32[512,128]{1,0:T(8,128)S(1)}, f32[512,128]{1,0:T(8,128)}, u32[]{:S(2)}) %copy-start) | copy-done | bytes 262168
  2.0 0.0 copy-start.1
  2.0 0.9 %copy-done.1 = bf16[2,256,256]{2,1,0:T(8,128)(2,1)S(1)} copy-done((bf16[2,256,256]{2,1,0:T(8,128)(2,1)S(1)}, bf16[2,256,256]{2,1,0:T(8,128)(2,1)}, u32[]{:S(2)}) %copy-start.1) | copy-done | bytes 262168
  2.9 0.0 copy-start.2
  2.9 0.9 %copy-done.2 = bf16[2,256,256]{2,1,0:T(8,128)(2,1)S(1)} copy-done((bf16[2,256,256]{2,1,0:T(8,128)(2,1)S(1)}, bf16[2,256,256]{2,1,0:T(8,128)(2,1)}, u32[]{:S(2)}) %copy-start.2) | copy-done | bytes 262168
  3.9 0.0 copy-start.4
  3.9 0.9 %copy-done.4 = bf16[512,128]{1,0:T(8,128)(2,1)S(1)} copy-done((bf16[512,128]{1,0:T(8,128)(2,1)S(1)}, bf16[512,128]{1,0:T(8,128)(2,1)}, u32[]{:S(2)}) %copy-start.4) | copy-done | bytes 131096
  4.8 0.0 copy-start.5
  4.8 0.9 %copy-done.5 = bf16[512,128]{1,0:T(8,128)(2,1)S(1)} copy-done((bf16[512,128]{1,0:T(8,128)(2,1)S(1)}, bf16[512,128]{1,0:T(8,128)(2,1)}, u32[]{:S(2)}) %copy-start.5) | copy-done | bytes 131096
  5.7 0.0 copy-start.7
  5.7 0.8 copy-done.7
  6.5 0.0 copy-start.8
  6.5 0.8 copy-done.8
  7.3 0.0 copy-start.10
  7.3 0.7 copy-done.10
  7.9 80.5 %hyena_mixer.1 = bf16[2,4,64,128]{3,2,1,0:T(8,128)(2,1)S(1)} custom-call(bf16[512,128]{1,0:T(8,128)(2,1)S(1)} %copy-done.3, bf16[512,128]{1,0:T(8,128)(2,1)S(1)} %copy-done.4, bf16[512,128]{1,0:T(8,128)(2,1)S(1)} %copy-done.5, f32[512,128]{1,0:T(8,128)S(1)} %copy-done, f32[1,512]{1,0:T(1,128)S(1)} %bitcast.4, bf16[512,64]{1,0:T(8,128)(2,1)S(1)} %copy.13.w_ref, ...), custom_call_target="tpu_custom_call" | custom-call | tf_op jit(solution)/shard_map/hyena_mixer/pallas_call | solution.py:354
  88.5 0.7 copy.15
Async XLA Ops:
  0.0 1.0 %copy-start.3 = (bf16[512,128]{1,0:T(8,128)(2,1)S(1)}, bf16[512,128]{1,0:T(8,128)(2,1)}, u32[]{:S(2)}) copy-start(bf16[512,128]{1,0:T(8,128)(2,1)} %q_ref.1) | copy-start | bytes 393220
  0.0 1.0 %copy-start.6 = (f32[2,64,128]{2,1,0:T(8,128)S(1)}, f32[2,64,128]{2,1,0:T(8,128)}, u32[]{:S(2)}) copy-start(f32[2,64,128]{2,1,0:T(8,128)} %constant.14.clone.turn_ref) | copy-start | bytes 196612
  0.0 1.0 %copy-start.9 = (f32[512]{0:T(512)S(1)}, f32[512]{0:T(512)}, u32[]{:S(2)}) copy-start(f32[512]{0:T(512)} %param.16) | copy-start | bytes 6148
  1.0 1.0 %copy-start = (f32[512,128]{1,0:T(8,128)S(1)}, f32[512,128]{1,0:T(8,128)}, u32[]{:S(2)}) copy-start(f32[512,128]{1,0:T(8,128)} %h_ref.1) | copy-start | bytes 786436
  2.0 0.9 %copy-start.1 = (bf16[2,256,256]{2,1,0:T(8,128)(2,1)S(1)}, bf16[2,256,256]{2,1,0:T(8,128)(2,1)}, u32[]{:S(2)}) copy-start(bf16[2,256,256]{2,1,0:T(8,128)(2,1)} %constant.12.clone.bwd_ref) | copy-start | bytes 786436
  2.9 0.9 %copy-start.2 = (bf16[2,256,256]{2,1,0:T(8,128)(2,1)S(1)}, bf16[2,256,256]{2,1,0:T(8,128)(2,1)}, u32[]{:S(2)}) copy-start(bf16[2,256,256]{2,1,0:T(8,128)(2,1)} %constant.11.clone.fwd_ref) | copy-start | bytes 786436
  3.9 0.9 %copy-start.4 = (bf16[512,128]{1,0:T(8,128)(2,1)S(1)}, bf16[512,128]{1,0:T(8,128)(2,1)}, u32[]{:S(2)}) copy-start(bf16[512,128]{1,0:T(8,128)(2,1)} %k_ref.1) | copy-start | bytes 393220
  4.8 0.9 %copy-start.5 = (bf16[512,128]{1,0:T(8,128)(2,1)S(1)}, bf16[512,128]{1,0:T(8,128)(2,1)}, u32[]{:S(2)}) copy-start(bf16[512,128]{1,0:T(8,128)(2,1)} %v_ref.1) | copy-start | bytes 393220
  5.7 0.8 copy-start.7
  6.5 0.8 copy-start.8
  7.3 0.7 copy-start.10

commit v2 on v1

v2 whole, which is shorter than its diff:
```python
import functools

import jax
import jax.numpy as jnp
import numpy as np
from jax import lax
from jax.experimental import pallas as pl
from jax.experimental.pallas import tpu as pltpu
from jax.sharding import PartitionSpec as P

F32 = jnp.float32
BF16 = jnp.bfloat16
MESH = pl.DeviceIdType.MESH
LANES = 128
GROUP = 8


def split_bf16(array):
    high = array.astype(BF16)
    low = (array - np.asarray(high, np.float64)).astype(BF16)
    return np.asarray(high), np.asarray(low)


def transform_tables(blocks):
    n1 = np.arange(blocks)[:, None]
    k1 = np.arange(blocks)[None, :] + 0.5
    outer = 2.0 * np.pi * n1 * k1 / (2 * blocks)
    first = np.concatenate([np.cos(outer).T, -np.sin(outer).T], 0)
    first_hi, first_lo = split_bf16(first)
    scale = 2.0 / (2 * blocks * LANES)
    last = np.concatenate([np.cos(outer), -np.sin(outer)], 1) * scale
    last_hi, last_lo = split_bf16(last)
    lane = np.arange(LANES)
    inner = 2.0 * np.pi * (lane[:, None] * lane[None, :] % LANES) / LANES
    cos_part, sin_part = np.cos(inner), -np.sin(inner)
    forward = np.block([[cos_part, sin_part], [-sin_part, cos_part]])
    backward = np.block([[cos_part, -sin_part], [sin_part, cos_part]])
    turn = 2.0 * np.pi * k1.T * lane[None, :] / (2 * blocks * LANES)
    return (
        np.concatenate([first_hi, first_lo], 1),
        np.stack(split_bf16(forward)),
        np.stack(split_bf16(backward)),
        np.concatenate([last_hi, last_lo, last_hi], 1),
        np.stack([np.cos(turn), -np.sin(turn)]).astype(np.float32),
    )


def dot(left, right):
    return jnp.dot(left, right, preferred_element_type=F32)


def halves(value):
    high = value.astype(BF16)
    return high, (value - high.astype(F32)).astype(BF16)


def dot_split(value, table_ref):
    high, low = halves(value)
    return dot(high, table_ref[0]) + dot(low, table_ref[0]) + dot(high, table_ref[1])


def column(row, targets):
    lanes = lax.broadcasted_iota(jnp.int32, (targets.shape[0], row.shape[1]), 1)
    return jnp.sum(jnp.where(lanes == targets, row, 0.0), axis=1, keepdims=True)


def kernel(
    dims,
    q_hbm,
    k_hbm,
    v_hbm,
    h_hbm,
    skip_hbm,
    w_hbm,
    bias_hbm,
    first_hbm,
    fwd_hbm,
    bwd_hbm,
    last_hbm,
    turn_hbm,
    out_ref,
    k_ref,
    v_ref,
    h_ref,
    skip_ref,
    bias_ref,
    first_ref,
    fwd_ref,
    bwd_ref,
    last_ref,
    turn_ref,
    cut,
    rows_in,
    query_in,
    seq_in,
    wide,
    conv_wide,
    conv_out,
    conv_in,
    gated_out,
    gated,
    w_line,
    weights,
    pair_out,
    pair_in,
    own_sum,
    sum_out,
    sum_in,
    load_sem,
    s_send,
    s_recv,
    q_send,
    q_recv,
    z_send,
    z_recv,
    wz_send,
    wz_recv,
    wp_send,
    wp_recv,
    r_send,
    r_recv,
    g_send,
    g_recv,
    c_send,
    c_recv,
    e_send,
    e_recv,
):
    zh_n, y_n, x_n, zl_n = dims
    plane = y_n * x_n
    blocks = zh_n * plane
    me = lax.axis_index("ctx")
    tp = lax.axis_index("tp")
    place = me % plane
    x = me % x_n
    y = place // x_n
    zh = me // plane
    core = tp % 2
    zl = tp // 2
    channels = k_hbm.shape[0]
    x_share = channels // x_n
    share = channels // plane
    width = w_hbm.shape[0]

    def device(zh_at, y_at, x_at, zl_at):
        return {"ctx": (zh_at * y_n + y_at) * x_n + x_at, "tp": zl_at * 2 + core}

    def in_plane(step):
        return {"ctx": zh * plane + (place + step) % plane, "tp": tp}

    def at_zh(step):
        return device((zh + step) % zh_n, y, x, zl)

    def at_x(step):
        return device(zh, y, (x + step) % x_n, zl)

    def at_y(step):
        return device(zh, (y + step) % y_n, x, zl)

    def at_row(y_step, z_step):
        return device(zh, (y + y_step) % y_n, x, (zl + z_step) % zl_n)

    other_core = {"ctx": me, "tp": zl * 2 + 1 - core}

    def remote(src, dst, send, recv, target):
        return pltpu.make_async_remote_copy(
            src_ref=src, dst_ref=dst, send_sem=send, recv_sem=recv, device_id=target, device_id_type=MESH
        )

    own_rows = pl.ds(pl.multiple_of(x * x_share + y * share, share), share)
    pairs = (
        (k_hbm, k_ref),
        (v_hbm, v_ref),
        (h_hbm, h_ref),
        (first_hbm, first_ref),
        (turn_hbm, turn_ref),
        (fwd_hbm, fwd_ref),
        (bwd_hbm, bwd_ref),
        (last_hbm, last_ref),
        (q_hbm.at[own_rows], query_in.at[place]),
        (skip_hbm, skip_ref),
        (bias_hbm, bias_ref),
    )
    loads = [pltpu.make_async_copy(src, dst, load_sem.at[n]) for n, (src, dst) in enumerate(pairs)]

    barrier = pltpu.get_barrier_semaphore()

    def greet(target):
        pl.semaphore_signal(barrier, inc=1, device_id=target, device_id_type=MESH)

    diagonal = zl == zh
    far_first = sorted(range(1, zh_n), key=lambda step: -min(step, zh_n - step))
    for step in far_first:
        greet(at_zh(step))
    for part in range(zl_n):

        @pl.when(jnp.logical_not(jnp.logical_and(diagonal, zl == part)))
        def _():
            greet(device(zl, y, x, part))

    for step in range(1, plane):
        greet(in_plane(step))
    for z_step in range(1, zl_n):
        for y_step in range(y_n):
            greet(at_row(y_step, z_step))
    greet(other_core)
    greeted = (zh_n - 1) + zl_n + (plane - 1) + (zl_n - 1) * y_n + 1

    for load in loads:
        load.start()
    for load in loads[:3]:
        load.wait()
    products = k_ref[...].astype(F32) * v_ref[...].astype(F32)
    pieces = jnp.concatenate(
        [products.reshape(blocks, GROUP, LANES), h_ref[...].reshape(blocks, GROUP, LANES)], 1
    ).astype(BF16)
    for x_at in range(x_n):
        for y_at in range(y_n):
            start = (x_at * y_n + y_at) * zh_n
            cut[y_at * x_n + x_at] = pieces[start : start + zh_n]
    pl.semaphore_wait(barrier, greeted - jnp.where(diagonal, 1, 0))

    s_copies = []
    for step in range(1, plane):
        copy = remote(
            cut.at[(place + step) % plane],
            rows_in.at[:, place],
            s_send.at[step],
            s_recv.at[step],
            in_plane(step),
        )
        copy.start()
        s_copies.append(copy)
    halves_at = [pl.ds(part * (width // 2), width // 2) for part in range(2)]
    wz_copies = [
        [
            remote(
                w_hbm.at[rows],
                w_line.at[zl, rows],
                wz_send.at[step, part],
                wz_recv.at[zl, part],
                device((zh + step) % zh_n, y, x, zh),
            )
            for part, rows in enumerate(halves_at)
        ]
        for step in range(zh_n)
    ]
    stay = [
        pltpu.make_async_copy(w_hbm.at[rows], w_line.at[zl, rows], wz_recv.at[zl, part])
        for part, rows in enumerate(halves_at)
    ]
    late = zh_n // 2
    for part in range(2):
        for step in [late] + [step for step in range(1, zh_n) if step != late]:
            if step != late or part == 0:
                wz_copies[step][part].start()

        @pl.when(diagonal)
        def _():
            stay[part].start()

        @pl.when(jnp.logical_not(diagonal))
        def _():
            wz_copies[0][part].start()

    def hand_on(part):
        for source in range(zl_n):
            block = w_line.at[source, halves_at[part]]
            pltpu.make_async_copy(block, block, wz_recv.at[source, part]).wait()
        sent = []
        for step in range(1, plane):
            columns = pl.ds(pl.multiple_of((place + step) % plane % x_n * x_share, x_share), x_share)
            copy = remote(
                w_line.at[:, halves_at[part], columns],
                weights.at[:, y, x, halves_at[part]],
                wp_send.at[step, part],
                wp_recv.at[step, part],
                in_plane(step),
            )
            copy.start()
            sent.append(copy)
        columns = pl.ds(pl.multiple_of(x * x_share, x_share), x_share)
        weights[:, y, x, halves_at[part]] = w_line[:, halves_at[part], columns]
        return sent

    rows_in[:, pl.ds(place, 1)] = cut[pl.ds(place, 1)].reshape(zh_n, 1, 2 * GROUP, LANES)
    for load in loads[3:]:
        load.wait()
    for copy in s_copies:
        copy.wait_recv()

    z_copies = []
    for step in far_first:
        copy = remote(
            rows_in.at[(zh + step) % zh_n], seq_in.at[zh], z_send.at[step], z_recv.at[step], at_zh(step)
        )
        copy.start()
        z_copies.append(copy)
    seq_in[zh] = rows_in[zh]
    q_copies = []
    for step in range(1, plane):
        target = (place + step) % plane
        rows = pl.ds(
            pl.multiple_of(target % x_n * x_share + target // x_n * share, share), share
        )
        copy = remote(
            q_hbm.at[rows], query_in.at[place], q_send.at[step], q_recv.at[step], in_plane(step)
        )
        copy.start()
        q_copies.append(copy)
    index = lax.broadcasted_iota(jnp.int32, (share, 1), 0)
    skip = column(skip_ref[...], x * x_share + y * share + index)
    wp_copies = hand_on(0)
    for copy in z_copies:
        copy.wait_recv()
    wz_copies[late][1].start()

    wide[...] = seq_in[...].reshape(blocks * 2 * GROUP, LANES).astype(F32)
    turn_re = turn_ref[0]
    turn_im = turn_ref[1]
    turn_re2 = jnp.concatenate([turn_re, turn_re], 1)
    turn_im2 = jnp.concatenate([turn_im, turn_im], 1)
    for channel in range(GROUP):
        signal = wide[pl.ds(channel, blocks, stride=2 * GROUP), :].astype(BF16)
        taps = wide[pl.ds(GROUP + channel, blocks, stride=2 * GROUP), :].astype(BF16)
        both = jnp.concatenate([signal, taps], 1)
        spread = dot(first_ref[...], jnp.concatenate([both, both], 0))
        re, im = spread[:blocks], spread[blocks:]
        turned_re = re * turn_re2 - im * turn_im2
        turned_im = re * turn_im2 + im * turn_re2
        stacked = jnp.concatenate(
            [
                jnp.concatenate([turned_re[:, :LANES], turned_im[:, :LANES]], 1),
                jnp.concatenate([turned_re[:, LANES:], turned_im[:, LANES:]], 1),
            ],
            0,
        )
        spectra = dot_split(stacked, fwd_ref)
        s_re, s_im = spectra[:blocks, :LANES], spectra[:blocks, LANES:]
        t_re, t_im = spectra[blocks:, :LANES], spectra[blocks:, LANES:]
        mixed = jnp.concatenate([s_re * t_re - s_im * t_im, s_re * t_im + s_im * t_re], 1)
        back = dot_split(mixed, bwd_ref)
        b_re, b_im = back[:, :LANES], back[:, LANES:]
        unturned = jnp.concatenate([b_re * turn_re + b_im * turn_im, b_im * turn_re - b_re * turn_im], 0)
        high, low = halves(unturned)
        conv_wide[pl.ds(channel, blocks, stride=GROUP), :] = dot(
            last_ref[...], jnp.concatenate([high, high, low], 0)
        )
    conv_out[...] = conv_wide[...].reshape(zh_n, plane, GROUP, LANES).astype(BF16)

    r_copies = []
    for step in far_first:
        copy = remote(
            conv_out.at[(zh + step) % zh_n], conv_in.at[zh], r_send.at[step], r_recv.at[step], at_zh(step)
        )
        copy.start()
        r_copies.append(copy)
    conv_in[zh] = conv_out[zh]

    wp_copies += hand_on(1)
    for copy in q_copies:
        copy.wait_recv()
    for copy in r_copies:
        copy.wait_recv()

    line_rows = pl.ds(pl.multiple_of(zl * x_share + y * share, share), share)
    offsets = sorted(range(1, x_n), key=lambda step: -min(step, x_n - step)) + [0]
    g_copies = []
    for turn, offset in enumerate(offsets):
        at = (x + offset) % x_n
        for y_at in range(y_n):
            spot = y_at * x_n + at
            long_conv = conv_in[:, pl.ds(spot, 1)].astype(F32).reshape(share, LANES)
            rows = rows_in[:, pl.ds(spot, 1)].astype(F32)[:, :, :GROUP].reshape(share, LANES)
            query = query_in[spot].astype(F32)
            gated_out[turn, y_at] = (query * (long_conv + skip * rows)).astype(BF16)
        sent = []
        for z_step in range(zl_n):
            for y_step in range(y_n):
                if z_step == 0 and y_step == 0:
                    continue
                copy = remote(
                    gated_out.at[turn, (y + y_step) % y_n],
                    gated.at[turn, line_rows],
                    g_send.at[turn, z_step, y_step],
                    g_recv.at[turn, z_step, y_step],
                    at_row(y_step, z_step),
                )
                copy.start()
                sent.append(copy)
        gated[turn, line_rows] = gated_out[turn, y]
        g_copies.append(sent)
    index = lax.broadcasted_iota(jnp.int32, (bias_ref.shape[1], 1), 0)
    bias = column(bias_ref[...], index)
    for copy in wp_copies:
        copy.wait_recv()

    half = y_n // 2

    def project(target, turn):
        blocks_at = pl.ds(target * half, half)
        block = jnp.concatenate(
            [weights[part, blocks_at].reshape(half * x_n * width, x_share) for part in range(zl_n)], 1
        )
        return dot(block, gated[turn])

    c_copies = []
    e_copies = []

    def pair_sum(turn):
        c_copies[turn].wait_recv()
        total = own_sum[turn] + pair_in[turn]
        if offsets[turn] == 0:
            return total
        sum_out[turn] = total.astype(BF16)
        copy = remote(
            sum_out.at[turn], sum_in.at[turn], e_send.at[turn], e_recv.at[turn], at_x(offsets[turn])
        )
        copy.start()
        e_copies.append(copy)

    for turn in range(x_n):
        for copy in g_copies[turn]:
            copy.wait_recv()
        pair_out[turn] = project(1 - core, turn)
        copy = remote(
            pair_out.at[turn], pair_in.at[turn], c_send.at[turn], c_recv.at[turn], other_core
        )
        copy.start()
        c_copies.append(copy)
        own_sum[turn] = project(core, turn)
        if turn:
            pair_sum(turn - 1)
    total = pair_sum(x_n - 1) + bias
    for turn in range(x_n - 1):
        e_copies[turn].wait_recv()
        total = total + sum_in[turn].astype(F32)
    out_ref[...] = total.astype(BF16)
    for copies in (s_copies, *wz_copies[1:], z_copies, q_copies, r_copies, wp_copies, c_copies, e_copies):
        for copy in copies:
            copy.wait_send()

    @pl.when(jnp.logical_not(diagonal))
    def _():
        for copy in wz_copies[0]:
            copy.wait_send()

    for sent in g_copies:
        for copy in sent:
            copy.wait_send()


def on_device(dims, query_gate, key_gate, value_input, long_filter, skip_gain, out_weight, out_bias):
    zh_n, y_n, x_n, zl_n = dims
    plane = y_n * x_n
    blocks = zh_n * plane
    channels = key_gate.shape[0]
    width = out_weight.shape[1]
    x_share = channels // x_n
    share = channels // plane
    outputs = out_bias.shape[0]
    tables = [jnp.asarray(table) for table in transform_tables(blocks)]
    dma = pltpu.SemaphoreType.DMA
    return pl.pallas_call(
        functools.partial(kernel, dims),
        out_shape=jax.ShapeDtypeStruct((outputs, LANES), BF16),
        in_specs=[pl.BlockSpec(memory_space=pltpu.HBM)] * 12,
        out_specs=pl.BlockSpec(memory_space=pltpu.VMEM),
        scratch_shapes=[
            pltpu.VMEM((channels, LANES), BF16),
            pltpu.VMEM((channels, LANES), BF16),
            pltpu.VMEM((channels, LANES), F32),
            pltpu.VMEM((1, channels), F32),
            pltpu.VMEM((1, outputs), F32),
            *[pltpu.VMEM(table.shape, table.dtype) for table in tables],
            pltpu.VMEM((plane, zh_n, 2 * GROUP, LANES), BF16),
            pltpu.VMEM((zh_n, plane, 2 * GROUP, LANES), BF16),
            pltpu.VMEM((plane, share, LANES), BF16),
            pltpu.VMEM((zh_n, plane, 2 * GROUP, LANES), BF16),
            pltpu.VMEM((blocks * 2 * GROUP, LANES), F32),
            pltpu.VMEM((blocks * GROUP, LANES), F32),
            pltpu.VMEM((zh_n, plane, GROUP, LANES), BF16),
            pltpu.VMEM((zh_n, plane, GROUP, LANES), BF16),
            pltpu.VMEM((x_n, y_n, share, LANES), BF16),
            pltpu.VMEM((x_n, channels, LANES), BF16),
            pltpu.VMEM((zl_n, width, channels), BF16),
            pltpu.VMEM((zl_n, y_n, x_n, width, x_share), BF16),
            pltpu.VMEM((x_n, outputs, LANES), F32),
            pltpu.VMEM((x_n, outputs, LANES), F32),
            pltpu.VMEM((x_n, outputs, LANES), F32),
            pltpu.VMEM((x_n, outputs, LANES), BF16),
            pltpu.VMEM((x_n, outputs, LANES), BF16),
            dma((11,)),
            dma((plane,)),
            dma((plane,)),
            dma((plane,)),
            dma((plane,)),
            dma((zh_n,)),
            dma((zh_n,)),
            dma((zh_n, 2)),
            dma((zl_n, 2)),
            dma((plane, 2)),
            dma((plane, 2)),
            dma((zh_n,)),
            dma((zh_n,)),
            dma((x_n, zl_n, y_n)),
            dma((x_n, zl_n, y_n)),
            dma((x_n,)),
            dma((x_n,)),
            dma((x_n,)),
            dma((x_n,)),
        ],
        compiler_params=pltpu.CompilerParams(
            collective_id=0, has_side_effects=True, vmem_limit_bytes=60 * 1024 * 1024
        ),
        name="hyena_mixer",
    )(
        query_gate,
        key_gate,
        value_input,
        long_filter,
        skip_gain.reshape(1, channels),
        out_weight.T,
        out_bias.reshape(1, -1),
        *tables,
    )


def solution(mesh, dims=(4, 4, 4, 4)):
    placed = (
        P("tp", "ctx"),
        P("tp", "ctx"),
        P("tp", "ctx"),
        P("tp", "ctx"),
        P("tp"),
        P("tp", "ctx"),
        P("tp"),
    )
    return jax.shard_map(
        functools.partial(on_device, dims),
        mesh=mesh,
        in_specs=placed,
        out_specs=P("tp", "ctx"),
        check_vma=False,
    )
```

time: 90.7 us -> 80.1 us (0.88); the launches traced: 89.2 us -> 79.9 us
  local copies, waits for them, and re-layouts: 8.55 us -> 1.57 us
  Pallas kernels: 80.5 us -> 78.4 us
    unnamed x24 -> x1, local copies, waits for them, and re-layouts: 8.55 us -> 1.57 us
    pallas_call x1, Pallas kernels: 80.5 us -> 78.4 us  [on_device(): pl.pallas_call(functools.partial(kernel, dims), out_shape=jax.ShapeDtypeS...]
where the time goes in v2:
time: 80.1 us; the launch traced here: 79.9 us
  Pallas kernels  78.4 us (98%)
  local copies, waits for them, and re-layouts  1.57 us (2%)
    pallas_call x1, Pallas kernels, on_device(): pl.pallas_call(functools.partial(kernel, dims), out_shape=jax.ShapeDtypeS...  78.4 us

profile of v2, /device:TPU:1, one launch (start us, length us, event | category | flops | bytes accessed | tf_op | source)
XLA Modules:
  0.0 79.9 jit_solution(4936922657396726166)
XLA Ops:
  0.0 78.4 %hyena_mixer.1 = bf16[512,128]{1,0:T(8,128)(2,1)} custom-call(bf16[512,128]{1,0:T(8,128)(2,1)} %q_hbm.1, bf16[512,128]{1,0:T(8,128)(2,1)} %k_hbm.1, bf16[512,128]{1,0:T(8,128)(2,1)} %v_hbm.1, f32[512,128]{1,0:T(8,128)} %h_hbm.1, f32[1,512]{1,0:T(1,128)} %bitcast.4, bf16[64,512]{1,0:T(8,128)(2,1)} %bitcast.3, f32[1,512]{1,0:T(1,128)} %bitcast.5, ...), custom_call_target="tpu_custom_call" | custom-call | tf_op jit(solution)/shard_map/hyena_mixer/pallas_call | solution.py:464
  78.4 1.6 %copy.14 = bf16[512,128]{1,0:T(8,128)(2,1)} copy(bf16[512,128]{1,0:T(8,128)(2,1)} %hyena_mixer.1) | data formatting | bytes 262144

commit v3 on v2

--- a/solution.py
+++ b/solution.py
@@ -57,6 +57,13 @@
 def dot_split(value, table_ref):
     high, low = halves(value)
     return dot(high, table_ref[0]) + dot(low, table_ref[0]) + dot(high, table_ref[1])
+
+
+def low_high(low, high, swap_low, swap_high):
+    row = lax.broadcasted_iota(jnp.int32, low.shape, low.ndim - 2)
+    low = pltpu.roll(low, GROUP // 2, low.ndim - 2) if swap_low else low
+    high = pltpu.roll(high, GROUP // 2, high.ndim - 2) if swap_high else high
+    return jnp.where(row < GROUP // 2, low, high)
 
 
 def column(row, targets):
@@ -92,7 +99,10 @@
     cut,
     rows_in,
     query_in,
+    line_cut,
     seq_in,
+    direct,
+    long_conv,
     wide,
     conv_wide,
     conv_out,
@@ -103,7 +113,6 @@
     weights,
     pair_out,
     pair_in,
-    own_sum,
     sum_out,
     sum_in,
     load_sem,
@@ -142,8 +151,9 @@
     share = channels // plane
     width = w_hbm.shape[0]
 
-    def device(zh_at, y_at, x_at, zl_at):
-        return {"ctx": (zh_at * y_n + y_at) * x_n + x_at, "tp": zl_at * 2 + core}
+    def device(zh_at, y_at, x_at, zl_at, core_at=None):
+        core_at = core if core_at is None else core_at
+        return {"ctx": (zh_at * y_n + y_at) * x_n + x_at, "tp": zl_at * 2 + core_at}
 
     def in_plane(step):
         return {"ctx": zh * plane + (place + step) % plane, "tp": tp}
@@ -203,34 +213,39 @@
     for z_step in range(1, zl_n):
         for y_step in range(y_n):
             greet(at_row(y_step, z_step))
-    greet(other_core)
-    greeted = (zh_n - 1) + zl_n + (plane - 1) + (zl_n - 1) * y_n + 1
+    for step in range(x_n):
+        greet(device(zh, y, (x + step) % x_n, zl, 1 - core))
+    greeted = (zh_n - 1) + zl_n + (plane - 1) + (zl_n - 1) * y_n + x_n
 
     for load in loads:
         load.start()
     for load in loads[:3]:
         load.wait()
-    products = k_ref[...].astype(F32) * v_ref[...].astype(F32)
-    pieces = jnp.concatenate(
-        [products.reshape(blocks, GROUP, LANES), h_ref[...].reshape(blocks, GROUP, LANES)], 1
-    ).astype(BF16)
-    for x_at in range(x_n):
-        for y_at in range(y_n):
-            start = (x_at * y_n + y_at) * zh_n
-            cut[y_at * x_n + x_at] = pieces[start : start + zh_n]
+    products = (k_ref[...].astype(F32) * v_ref[...].astype(F32)).reshape(blocks, GROUP, LANES)
+    taps = h_ref[...].reshape(blocks, GROUP, LANES)
+    pieces = (low_high(products, taps, False, True), low_high(products, taps, True, False))
+    for part in range(2):
+        packed = pieces[part].reshape(blocks // 2, 2 * GROUP, LANES).astype(BF16)
+        for x_at in range(x_n):
+            for y_at in range(y_n):
+                start = (x_at * y_n + y_at) * zh_n // 2
+                cut[part, y_at * x_n + x_at] = packed[start : start + zh_n // 2]
     pl.semaphore_wait(barrier, greeted - jnp.where(diagonal, 1, 0))
 
     s_copies = []
-    for step in range(1, plane):
-        copy = remote(
-            cut.at[(place + step) % plane],
-            rows_in.at[:, place],
-            s_send.at[step],
-            s_recv.at[step],
-            in_plane(step),
-        )
-        copy.start()
-        s_copies.append(copy)
+    for part in range(2):
+        sent = []
+        for step in range(1, plane):
+            copy = remote(
+                cut.at[part, (place + step) % plane],
+                rows_in.at[part, :, place],
+                s_send.at[step, part],
+                s_recv.at[step, part],
+                in_plane(step),
+            )
+            copy.start()
+            sent.append(copy)
+        s_copies.append(sent)
     halves_at = [pl.ds(part * (width // 2), width // 2) for part in range(2)]
     wz_copies = [
         [
@@ -250,9 +265,13 @@
         for part, rows in enumerate(halves_at)
     ]
     late = zh_n // 2
-    for part in range(2):
-        for step in [late] + [step for step in range(1, zh_n) if step != late]:
-            if step != late or part == 0:
+
+    def send_far(part):
+        wz_copies[late][part].start()
+
+    def send_near(part):
+        for step in range(1, zh_n):
+            if step != late:
                 wz_copies[step][part].start()
 
         @pl.when(diagonal)
@@ -262,6 +281,9 @@
         @pl.when(jnp.logical_not(diagonal))
         def _():
             wz_copies[0][part].start()
+
+    send_far(0)
+    send_near(0)
 
     def hand_on(part):
         for source in range(zl_n):
@@ -283,20 +305,42 @@
         weights[:, y, x, halves_at[part]] = w_line[:, halves_at[part], columns]
         return sent
 
-    rows_in[:, pl.ds(place, 1)] = cut[pl.ds(place, 1)].reshape(zh_n, 1, 2 * GROUP, LANES)
+    for part in range(2):
+        rows_in[part, :, pl.ds(place, 1)] = cut[part, pl.ds(place, 1)].reshape(
+            zh_n // 2, 1, 2 * GROUP, LANES
+        )
     for load in loads[3:]:
         load.wait()
-    for copy in s_copies:
-        copy.wait_recv()
-
+
+    index = lax.broadcasted_iota(jnp.int32, (share, 1), 0)
+    skip = column(skip_ref[...], x * x_share + y * share + index).reshape(zh_n, 1, GROUP, 1)
     z_copies = []
-    for step in far_first:
-        copy = remote(
-            rows_in.at[(zh + step) % zh_n], seq_in.at[zh], z_send.at[step], z_recv.at[step], at_zh(step)
-        )
-        copy.start()
-        z_copies.append(copy)
-    seq_in[zh] = rows_in[zh]
+    arrived = []
+    for part in range(2):
+        for copy in s_copies[part]:
+            copy.wait_recv()
+        value = rows_in[part].astype(F32).reshape(zh_n // 2, plane, 2, GROUP, LANES)
+        arrived.append(value)
+        for zh_at in range(zh_n):
+            line_cut[part, zh_at] = (
+                value[zh_at // 2, :, zh_at % 2].reshape(plane // 2, 2 * GROUP, LANES).astype(BF16)
+            )
+        sent = []
+        for step in far_first:
+            copy = remote(
+                line_cut.at[part, (zh + step) % zh_n],
+                seq_in.at[part, zh],
+                z_send.at[step, part],
+                z_recv.at[step, part],
+                at_zh(step),
+            )
+            copy.start()
+            sent.append(copy)
+        seq_in[part, pl.ds(zh, 1)] = line_cut[part, pl.ds(zh, 1)]
+        z_copies.append(sent)
+    for zh_at in range(zh_n):
+        first, second = (value[zh_at // 2, :, zh_at % 2] for value in arrived)
+        direct[:, zh_at] = skip[zh_at] * low_high(first, second, False, True)
     q_copies = []
     for step in range(1, plane):
         target = (place + step) % plane
@@ -308,60 +352,68 @@
         )
         copy.start()
         q_copies.append(copy)
-    index = lax.broadcasted_iota(jnp.int32, (share, 1), 0)
-    skip = column(skip_ref[...], x * x_share + y * share + index)
     wp_copies = hand_on(0)
-    for copy in z_copies:
-        copy.wait_recv()
-    wz_copies[late][1].start()
-
-    wide[...] = seq_in[...].reshape(blocks * 2 * GROUP, LANES).astype(F32)
     turn_re = turn_ref[0]
     turn_im = turn_ref[1]
     turn_re2 = jnp.concatenate([turn_re, turn_re], 1)
     turn_im2 = jnp.concatenate([turn_im, turn_im], 1)
-    for channel in range(GROUP):
-        signal = wide[pl.ds(channel, blocks, stride=2 * GROUP), :].astype(BF16)
-        taps = wide[pl.ds(GROUP + channel, blocks, stride=2 * GROUP), :].astype(BF16)
-        both = jnp.concatenate([signal, taps], 1)
-        spread = dot(first_ref[...], jnp.concatenate([both, both], 0))
-        re, im = spread[:blocks], spread[blocks:]
-        turned_re = re * turn_re2 - im * turn_im2
-        turned_im = re * turn_im2 + im * turn_re2
-        stacked = jnp.concatenate(
-            [
-                jnp.concatenate([turned_re[:, :LANES], turned_im[:, :LANES]], 1),
-                jnp.concatenate([turned_re[:, LANES:], turned_im[:, LANES:]], 1),
-            ],
-            0,
-        )
-        spectra = dot_split(stacked, fwd_ref)
-        s_re, s_im = spectra[:blocks, :LANES], spectra[:blocks, LANES:]
-        t_re, t_im = spectra[blocks:, :LANES], spectra[blocks:, LANES:]
-        mixed = jnp.concatenate([s_re * t_re - s_im * t_im, s_re * t_im + s_im * t_re], 1)
-        back = dot_split(mixed, bwd_ref)
-        b_re, b_im = back[:, :LANES], back[:, LANES:]
-        unturned = jnp.concatenate([b_re * turn_re + b_im * turn_im, b_im * turn_re - b_re * turn_im], 0)
-        high, low = halves(unturned)
-        conv_wide[pl.ds(channel, blocks, stride=GROUP), :] = dot(
-            last_ref[...], jnp.concatenate([high, high, low], 0)
-        )
-    conv_out[...] = conv_wide[...].reshape(zh_n, plane, GROUP, LANES).astype(BF16)
-
     r_copies = []
-    for step in far_first:
-        copy = remote(
-            conv_out.at[(zh + step) % zh_n], conv_in.at[zh], r_send.at[step], r_recv.at[step], at_zh(step)
-        )
-        copy.start()
-        r_copies.append(copy)
-    conv_in[zh] = conv_out[zh]
-
+    for part in range(2):
+        for copy in z_copies[part]:
+            copy.wait_recv()
+        if part:
+            send_far(1)
+        wide[part] = seq_in[part].astype(F32).reshape(blocks * GROUP, LANES)
+        for channel in range(GROUP // 2):
+            signal = wide[part, pl.ds(channel, blocks, stride=GROUP), :].astype(BF16)
+            taps = wide[part, pl.ds(GROUP // 2 + channel, blocks, stride=GROUP), :].astype(BF16)
+            both = jnp.concatenate([signal, taps], 1)
+            spread = dot(first_ref[...], jnp.concatenate([both, both], 0))
+            re, im = spread[:blocks], spread[blocks:]
+            turned_re = re * turn_re2 - im * turn_im2
+            turned_im = re * turn_im2 + im * turn_re2
+            stacked = jnp.concatenate(
+                [
+                    jnp.concatenate([turned_re[:, :LANES], turned_im[:, :LANES]], 1),
+                    jnp.concatenate([turned_re[:, LANES:], turned_im[:, LANES:]], 1),
+                ],
+                0,
+            )
+            spectra = dot_split(stacked, fwd_ref)
+            s_re, s_im = spectra[:blocks, :LANES], spectra[:blocks, LANES:]
+            t_re, t_im = spectra[blocks:, :LANES], spectra[blocks:, LANES:]
+            mixed = jnp.concatenate([s_re * t_re - s_im * t_im, s_re * t_im + s_im * t_re], 1)
+            back = dot_split(mixed, bwd_ref)
+            b_re, b_im = back[:, :LANES], back[:, LANES:]
+            unturned = jnp.concatenate([b_re * turn_re + b_im * turn_im, b_im * turn_re - b_re * turn_im], 0)
+            high, low = halves(unturned)
+            conv_wide[part, pl.ds(channel, blocks, stride=GROUP // 2), :] = dot(
+                last_ref[...], jnp.concatenate([high, high, low], 0)
+            )
+        conv_out[part] = conv_wide[part].reshape(zh_n, plane * GROUP // 2, LANES).astype(BF16)
+        for step in far_first:
+            copy = remote(
+                conv_out.at[part, (zh + step) % zh_n],
+                conv_in.at[part, zh],
+                r_send.at[step, part],
+                r_recv.at[step, part],
+                at_zh(step),
+            )
+            copy.start()
+            r_copies.append(copy)
+        conv_in[part, pl.ds(zh, 1)] = conv_out[part, pl.ds(zh, 1)]
+    send_near(1)
     wp_copies += hand_on(1)
     for copy in q_copies:
         copy.wait_recv()
     for copy in r_copies:
         copy.wait_recv()
+    first, second = (
+        conv_in[part].astype(F32).reshape(zh_n, plane // 2, GROUP, LANES) for part in range(2)
+    )
+    for spot in range(plane):
+        odd = spot % 2 == 1
+        long_conv[spot] = direct[spot] + low_high(first[:, spot // 2], second[:, spot // 2], odd, not odd)
 
     line_rows = pl.ds(pl.multiple_of(zl * x_share + y * share, share), share)
     offsets = sorted(range(1, x_n), key=lambda step: -min(step, x_n - step)) + [0]
@@ -370,10 +422,8 @@
         at = (x + offset) % x_n
         for y_at in range(y_n):
             spot = y_at * x_n + at
-            long_conv = conv_in[:, pl.ds(spot, 1)].astype(F32).reshape(share, LANES)
-            rows = rows_in[:, pl.ds(spot, 1)].astype(F32)[:, :, :GROUP].reshape(share, LANES)
             query = query_in[spot].astype(F32)
-            gated_out[turn, y_at] = (query * (long_conv + skip * rows)).astype(BF16)
+            gated_out[turn, y_at] = (query * long_conv[spot].reshape(share, LANES)).astype(BF16)
         sent = []
         for z_step in range(zl_n):
             for y_step in range(y_n):
@@ -404,39 +454,35 @@
         )
         return dot(block, gated[turn])
 
-    c_copies = []
     e_copies = []
-
-    def pair_sum(turn):
-        c_copies[turn].wait_recv()
-        total = own_sum[turn] + pair_in[turn]
-        if offsets[turn] == 0:
-            return total
-        sum_out[turn] = total.astype(BF16)
-        copy = remote(
-            sum_out.at[turn], sum_in.at[turn], e_send.at[turn], e_recv.at[turn], at_x(offsets[turn])
-        )
-        copy.start()
-        e_copies.append(copy)
-
-    for turn in range(x_n):
+    for turn in range(x_n - 1):
         for copy in g_copies[turn]:
             copy.wait_recv()
-        pair_out[turn] = project(1 - core, turn)
-        copy = remote(
-            pair_out.at[turn], pair_in.at[turn], c_send.at[turn], c_recv.at[turn], other_core
-        )
-        copy.start()
-        c_copies.append(copy)
-        own_sum[turn] = project(core, turn)
-        if turn:
-            pair_sum(turn - 1)
-    total = pair_sum(x_n - 1) + bias
+        for side in range(2):
+            sum_out[turn, side] = project((core + side) % 2, turn).astype(BF16)
+            copy = remote(
+                sum_out.at[turn, side],
+                sum_in.at[turn, side],
+                e_send.at[turn, side],
+                e_recv.at[turn, side],
+                device(zh, y, (x + offsets[turn]) % x_n, zl, (core + side) % 2),
+            )
+            copy.start()
+            e_copies.append(copy)
+    for copy in g_copies[x_n - 1]:
+        copy.wait_recv()
+    pair_out[...] = project(1 - core, x_n - 1)
+    pair_copy = remote(pair_out, pair_in, c_send, c_recv, other_core)
+    pair_copy.start()
+    total = project(core, x_n - 1) + bias
     for turn in range(x_n - 1):
-        e_copies[turn].wait_recv()
-        total = total + sum_in[turn].astype(F32)
+        for side in range(2):
+            e_copies[2 * turn + side].wait_recv()
+            total = total + sum_in[turn, side].astype(F32)
+    pair_copy.wait_recv()
+    total = total + pair_in[...]
     out_ref[...] = total.astype(BF16)
-    for copies in (s_copies, *wz_copies[1:], z_copies, q_copies, r_copies, wp_copies, c_copies, e_copies):
+    for copies in (*s_copies, *wz_copies[1:], *z_copies, q_copies, r_copies, wp_copies, [pair_copy], e_copies):
         for copy in copies:
             copy.wait_send()
 
@@ -473,42 +519,44 @@
             pltpu.VMEM((1, channels), F32),
             pltpu.VMEM((1, outputs), F32),
             *[pltpu.VMEM(table.shape, table.dtype) for table in tables],
-            pltpu.VMEM((plane, zh_n, 2 * GROUP, LANES), BF16),
-            pltpu.VMEM((zh_n, plane, 2 * GROUP, LANES), BF16),
+            pltpu.VMEM((2, plane, zh_n // 2, 2 * GROUP, LANES), BF16),
+            pltpu.VMEM((2, zh_n // 2, plane, 2 * GROUP, LANES), BF16),
             pltpu.VMEM((plane, share, LANES), BF16),
-            pltpu.VMEM((zh_n, plane, 2 * GROUP, LANES), BF16),
-            pltpu.VMEM((blocks * 2 * GROUP, LANES), F32),
-            pltpu.VMEM((blocks * GROUP, LANES), F32),
-            pltpu.VMEM((zh_n, plane, GROUP, LANES), BF16),
-            pltpu.VMEM((zh_n, plane, GROUP, LANES), BF16),
+            pltpu.VMEM((2, zh_n, plane // 2, 2 * GROUP, LANES), BF16),
+            pltpu.VMEM((2, zh_n, plane // 2, 2 * GROUP, LANES), BF16),
+            pltpu.VMEM((plane, zh_n, GROUP, LANES), F32),
+            pltpu.VMEM((plane, zh_n, GROUP, LANES), F32),
+            pltpu.VMEM((2, blocks * GROUP, LANES), F32),
+            pltpu.VMEM((2, blocks * GROUP // 2, LANES), F32),
+            pltpu.VMEM((2, zh_n, plane * GROUP // 2, LANES), BF16),
+            pltpu.VMEM((2, zh_n, plane * GROUP // 2, LANES), BF16),
             pltpu.VMEM((x_n, y_n, share, LANES), BF16),
             pltpu.VMEM((x_n, channels, LANES), BF16),
             pltpu.VMEM((zl_n, width, channels), BF16),
             pltpu.VMEM((zl_n, y_n, x_n, width, x_share), BF16),
-            pltpu.VMEM((x_n, outputs, LANES), F32),
-            pltpu.VMEM((x_n, outputs, LANES), F32),
-            pltpu.VMEM((x_n, outputs, LANES), F32),
-            pltpu.VMEM((x_n, outputs, LANES), BF16),
-            pltpu.VMEM((x_n, outputs, LANES), BF16),
+            pltpu.VMEM((outputs, LANES), F32),
+            pltpu.VMEM((outputs, LANES), F32),
+            pltpu.VMEM((x_n - 1, 2, outputs, LANES), BF16),
+            pltpu.VMEM((x_n - 1, 2, outputs, LANES), BF16),
             dma((11,)),
+            dma((plane, 2)),
+            dma((plane, 2)),
             dma((plane,)),
             dma((plane,)),
-            dma((plane,)),
-            dma((plane,)),
-            dma((zh_n,)),
-            dma((zh_n,)),
+            dma((zh_n, 2)),
+            dma((zh_n, 2)),
             dma((zh_n, 2)),
             dma((zl_n, 2)),
             dma((plane, 2)),
             dma((plane, 2)),
-            dma((zh_n,)),
-            dma((zh_n,)),
+            dma((zh_n, 2)),
+            dma((zh_n, 2)),
             dma((x_n, zl_n, y_n)),
             dma((x_n, zl_n, y_n)),
-            dma((x_n,)),
-            dma((x_n,)),
-            dma((x_n,)),
-            dma((x_n,)),
+            dma,
+            dma,
+            dma((x_n - 1, 2)),
+            dma((x_n - 1, 2)),
         ],
         compiler_params=pltpu.CompilerParams(
             collective_id=0, has_side_effects=True, vmem_limit_bytes=60 * 1024 * 1024

time: 80.1 us -> 83.4 us (1.041)
  the two profiles are of different devices: /device:TPU:1 before, /device:TPU:33 now
where the time goes in v3:
time: 83.4 us; the launch traced here: 83.2 us
  Pallas kernels  81.6 us (98%)
  local copies, waits for them, and re-layouts  1.57 us (2%)
    pallas_call x1, Pallas kernels, on_device(): pl.pallas_call(functools.partial(kernel, dims), out_shape=jax.ShapeDtypeS...  81.6 us

profile of v3, /device:TPU:33, one launch (start us, length us, event | category | flops | bytes accessed | tf_op | source)
XLA Modules:
  0.0 83.2 jit_solution(9295102319153307018)
XLA Ops:
  0.0 81.6 %hyena_mixer.1 = bf16[512,128]{1,0:T(8,128)(2,1)} custom-call(bf16[512,128]{1,0:T(8,128)(2,1)} %q_hbm.1, bf16[512,128]{1,0:T(8,128)(2,1)} %k_hbm.1, bf16[512,128]{1,0:T(8,128)(2,1)} %v_hbm.1, f32[512,128]{1,0:T(8,128)} %h_hbm.1, f32[1,512]{1,0:T(1,128)} %bitcast.4, bf16[64,512]{1,0:T(8,128)(2,1)} %bitcast.3, f32[1,512]{1,0:T(1,128)} %bitcast.5, ...), custom_call_target="tpu_custom_call" | custom-call | tf_op jit(solution)/shard_map/hyena_mixer/pallas_call | solution.py:510
  81.6 1.6 %copy.14 = bf16[512,128]{1,0:T(8,128)(2,1)} copy(bf16[512,128]{1,0:T(8,128)(2,1)} %hyena_mixer.1) | data formatting | bytes 262144

commit v4 on v3

--- a/solution.py
+++ b/solution.py
@@ -123,7 +123,8 @@
     z_send,
     z_recv,
     wz_send,
-    wz_recv,
+    wf_send,
+    w_recv,
     wp_send,
     wp_recv,
     r_send,
@@ -199,12 +200,20 @@
         pl.semaphore_signal(barrier, inc=1, device_id=target, device_id_type=MESH)
 
     diagonal = zl == zh
+    apart = (zh - zl + zh_n) % zh_n
+    last = zh_n - 1
     far_first = sorted(range(1, zh_n), key=lambda step: -min(step, zh_n - step))
+
+    def direct_piece(part):
+        above = jnp.logical_and(apart == 1, zl <= part)
+        below = jnp.logical_and(apart == last, zl >= part)
+        return jnp.logical_or(apart == 0, jnp.logical_or(above, below))
+
     for step in far_first:
         greet(at_zh(step))
     for part in range(zl_n):
 
-        @pl.when(jnp.logical_not(jnp.logical_and(diagonal, zl == part)))
+        @pl.when(jnp.logical_and(zl != part, direct_piece(part)))
         def _():
             greet(device(zl, y, x, part))
 
@@ -213,9 +222,8 @@
     for z_step in range(1, zl_n):
         for y_step in range(y_n):
             greet(at_row(y_step, z_step))
-    for step in range(x_n):
-        greet(device(zh, y, (x + step) % x_n, zl, 1 - core))
-    greeted = (zh_n - 1) + zl_n + (plane - 1) + (zl_n - 1) * y_n + x_n
+    greet(other_core)
+    greeted = (zh_n - 1) + (plane - 1) + (zl_n - 1) * y_n + 1
 
     for load in loads:
         load.start()
@@ -230,7 +238,7 @@
             for y_at in range(y_n):
                 start = (x_at * y_n + y_at) * zh_n // 2
                 cut[part, y_at * x_n + x_at] = packed[start : start + zh_n // 2]
-    pl.semaphore_wait(barrier, greeted - jnp.where(diagonal, 1, 0))
+    pl.semaphore_wait(barrier, greeted + jnp.where(diagonal, 0, 2))
 
     s_copies = []
     for part in range(2):
@@ -246,64 +254,72 @@
             copy.start()
             sent.append(copy)
         s_copies.append(sent)
-    halves_at = [pl.ds(part * (width // 2), width // 2) for part in range(2)]
-    wz_copies = [
-        [
-            remote(
-                w_hbm.at[rows],
-                w_line.at[zl, rows],
-                wz_send.at[step, part],
-                wz_recv.at[zl, part],
-                device((zh + step) % zh_n, y, x, zh),
-            )
-            for part, rows in enumerate(halves_at)
-        ]
-        for step in range(zh_n)
-    ]
-    stay = [
-        pltpu.make_async_copy(w_hbm.at[rows], w_line.at[zl, rows], wz_recv.at[zl, part])
-        for part, rows in enumerate(halves_at)
-    ]
-    late = zh_n // 2
-
-    def send_far(part):
-        wz_copies[late][part].start()
-
-    def send_near(part):
-        for step in range(1, zh_n):
-            if step != late:
-                wz_copies[step][part].start()
-
-        @pl.when(diagonal)
+    def own_piece(slot, step):
+        return remote(
+            w_hbm, w_line.at[zl], wz_send.at[slot], w_recv.at[zl], device((zh + step) % zh_n, y, x, zh)
+        )
+
+    source_copies = (
+        (zl >= zh, own_piece(0, 1)),
+        (zl <= zh, own_piece(1, last)),
+        (jnp.logical_not(diagonal), own_piece(2, 0)),
+    )
+    stay = pltpu.make_async_copy(w_hbm, w_line.at[zl], w_recv.at[zl])
+    for when, copy in source_copies:
+
+        @pl.when(when)
         def _():
-            stay[part].start()
-
-        @pl.when(jnp.logical_not(diagonal))
-        def _():
-            wz_copies[0][part].start()
-
-    send_far(0)
-    send_near(0)
-
-    def hand_on(part):
-        for source in range(zl_n):
-            block = w_line.at[source, halves_at[part]]
-            pltpu.make_async_copy(block, block, wz_recv.at[source, part]).wait()
+            copy.start()
+
+    @pl.when(diagonal)
+    def _():
+        stay.start()
+
+    def relay(part, step, slot, rows=slice(None)):
+        piece = w_line.at[part, rows]
+        return remote(piece, piece, wf_send.at[slot[0], slot[1]], w_recv.at[part], at_zh(step))
+
+    relay_copies = []
+    for part in range(zl_n):
+        inner = jnp.logical_and(apart == 0, zl != part)
+        for up in range(2):
+            step = 1 if up else last
+            side = (zl > part) if up else (zl < part)
+            relay_copies.append((jnp.logical_and(inner, side), relay(part, step, (part, up))))
+        for up in range(2):
+            step = 1 if up else last
+            outer = apart == (1 if up else last)
+            side = (zl < part) if up else (zl > part)
+            rows = pl.ds(0, width // 2) if up else pl.ds(width // 2, width // 2)
+            relay_copies.append((jnp.logical_and(outer, side), relay(part, step, (part, up))))
+            relay_copies.append(
+                (jnp.logical_and(outer, zl == part), relay(part, step, (part, up), rows))
+            )
+
+    wp_copies = []
+    for part in range(zl_n):
         sent = []
         for step in range(1, plane):
             columns = pl.ds(pl.multiple_of((place + step) % plane % x_n * x_share, x_share), x_share)
-            copy = remote(
-                w_line.at[:, halves_at[part], columns],
-                weights.at[:, y, x, halves_at[part]],
-                wp_send.at[step, part],
-                wp_recv.at[step, part],
-                in_plane(step),
-            )
+            sent.append(
+                remote(
+                    w_line.at[part, :, columns],
+                    weights.at[part, y, x],
+                    wp_send.at[part, step],
+                    wp_recv.at[part, step],
+                    in_plane(step),
+                )
+            )
+        wp_copies.append(sent)
+
+    def piece_in(part):
+        pltpu.make_async_copy(w_line.at[part], w_line.at[part], w_recv.at[part]).wait()
+
+    def hand_on(part):
+        for copy in wp_copies[part]:
             copy.start()
-            sent.append(copy)
         columns = pl.ds(pl.multiple_of(x * x_share, x_share), x_share)
-        weights[:, y, x, halves_at[part]] = w_line[:, halves_at[part], columns]
-        return sent
+        weights[part, y, x] = w_line[part, :, columns]
 
     for part in range(2):
         rows_in[part, :, pl.ds(place, 1)] = cut[part, pl.ds(place, 1)].reshape(
@@ -352,7 +368,25 @@
         )
         copy.start()
         q_copies.append(copy)
-    wp_copies = hand_on(0)
+
+    for part in range(zl_n):
+
+        @pl.when(direct_piece(part))
+        def _():
+            piece_in(part)
+
+    for when, copy in relay_copies:
+
+        @pl.when(when)
+        def _():
+            copy.start()
+
+    for part in range(zl_n):
+
+        @pl.when(direct_piece(part))
+        def _():
+            hand_on(part)
+
     turn_re = turn_ref[0]
     turn_im = turn_ref[1]
     turn_re2 = jnp.concatenate([turn_re, turn_re], 1)
@@ -361,35 +395,41 @@
     for part in range(2):
         for copy in z_copies[part]:
             copy.wait_recv()
-        if part:
-            send_far(1)
         wide[part] = seq_in[part].astype(F32).reshape(blocks * GROUP, LANES)
-        for channel in range(GROUP // 2):
+        group = range(GROUP // 2)
+        spread = []
+        for channel in group:
             signal = wide[part, pl.ds(channel, blocks, stride=GROUP), :].astype(BF16)
             taps = wide[part, pl.ds(GROUP // 2 + channel, blocks, stride=GROUP), :].astype(BF16)
             both = jnp.concatenate([signal, taps], 1)
-            spread = dot(first_ref[...], jnp.concatenate([both, both], 0))
-            re, im = spread[:blocks], spread[blocks:]
+            spread.append(dot(first_ref[...], jnp.concatenate([both, both], 0)))
+        stacked = []
+        for value in spread:
+            re, im = value[:blocks], value[blocks:]
             turned_re = re * turn_re2 - im * turn_im2
             turned_im = re * turn_im2 + im * turn_re2
-            stacked = jnp.concatenate(
-                [
-                    jnp.concatenate([turned_re[:, :LANES], turned_im[:, :LANES]], 1),
-                    jnp.concatenate([turned_re[:, LANES:], turned_im[:, LANES:]], 1),
-                ],
-                0,
-            )
-            spectra = dot_split(stacked, fwd_ref)
-            s_re, s_im = spectra[:blocks, :LANES], spectra[:blocks, LANES:]
-            t_re, t_im = spectra[blocks:, :LANES], spectra[blocks:, LANES:]
-            mixed = jnp.concatenate([s_re * t_re - s_im * t_im, s_re * t_im + s_im * t_re], 1)
-            back = dot_split(mixed, bwd_ref)
-            b_re, b_im = back[:, :LANES], back[:, LANES:]
-            unturned = jnp.concatenate([b_re * turn_re + b_im * turn_im, b_im * turn_re - b_re * turn_im], 0)
-            high, low = halves(unturned)
-            conv_wide[part, pl.ds(channel, blocks, stride=GROUP // 2), :] = dot(
-                last_ref[...], jnp.concatenate([high, high, low], 0)
-            )
+            stacked.append(jnp.concatenate([turned_re[:, :LANES], turned_im[:, :LANES]], 1))
+            stacked.append(jnp.concatenate([turned_re[:, LANES:], turned_im[:, LANES:]], 1))
+        spectra = dot_split(jnp.concatenate(stacked, 0), fwd_ref)
+        mixed = []
+        for channel in group:
+            one = spectra[2 * channel * blocks : (2 * channel + 1) * blocks]
+            two = spectra[(2 * channel + 1) * blocks : (2 * channel + 2) * blocks]
+            s_re, s_im, t_re, t_im = one[:, :LANES], one[:, LANES:], two[:, :LANES], two[:, LANES:]
+            mixed.append(jnp.concatenate([s_re * t_re - s_im * t_im, s_re * t_im + s_im * t_re], 1))
+        back = dot_split(jnp.concatenate(mixed, 0), bwd_ref)
+        unturned = []
+        for channel in group:
+            one = back[channel * blocks : (channel + 1) * blocks]
+            b_re, b_im = one[:, :LANES], one[:, LANES:]
+            unturned.append(
+                jnp.concatenate([b_re * turn_re + b_im * turn_im, b_im * turn_re - b_re * turn_im], 0)
+            )
+        for channel in range(0, GROUP // 2, 2):
+            high, low = halves(jnp.concatenate(unturned[channel : channel + 2], 1))
+            result = dot(last_ref[...], jnp.concatenate([high, high, low], 0))
+            conv_wide[part, pl.ds(channel, blocks, stride=GROUP // 2), :] = result[:, :LANES]
+            conv_wide[part, pl.ds(channel + 1, blocks, stride=GROUP // 2), :] = result[:, LANES:]
         conv_out[part] = conv_wide[part].reshape(zh_n, plane * GROUP // 2, LANES).astype(BF16)
         for step in far_first:
             copy = remote(
@@ -402,8 +442,14 @@
             copy.start()
             r_copies.append(copy)
         conv_in[part, pl.ds(zh, 1)] = conv_out[part, pl.ds(zh, 1)]
-    send_near(1)
-    wp_copies += hand_on(1)
+
+    for part in range(zl_n):
+
+        @pl.when(jnp.logical_not(direct_piece(part)))
+        def _():
+            piece_in(part)
+            hand_on(part)
+
     for copy in q_copies:
         copy.wait_recv()
     for copy in r_copies:
@@ -442,8 +488,9 @@
         g_copies.append(sent)
     index = lax.broadcasted_iota(jnp.int32, (bias_ref.shape[1], 1), 0)
     bias = column(bias_ref[...], index)
-    for copy in wp_copies:
-        copy.wait_recv()
+    for sent in wp_copies:
+        for copy in sent:
+            copy.wait_recv()
 
     half = y_n // 2
 
@@ -454,41 +501,40 @@
         )
         return dot(block, gated[turn])
 
+    c_copies = []
     e_copies = []
-    for turn in range(x_n - 1):
+    for turn in range(x_n):
         for copy in g_copies[turn]:
             copy.wait_recv()
-        for side in range(2):
-            sum_out[turn, side] = project((core + side) % 2, turn).astype(BF16)
+        pair_out[turn] = project(1 - core, turn)
+        pair_copy = remote(
+            pair_out.at[turn], pair_in.at[turn], c_send.at[turn], c_recv.at[turn], other_core
+        )
+        pair_copy.start()
+        c_copies.append(pair_copy)
+        total = project(core, turn)
+        pair_copy.wait_recv()
+        total = total + pair_in[turn]
+        if turn < x_n - 1:
+            sum_out[turn] = total.astype(BF16)
             copy = remote(
-                sum_out.at[turn, side],
-                sum_in.at[turn, side],
-                e_send.at[turn, side],
-                e_recv.at[turn, side],
-                device(zh, y, (x + offsets[turn]) % x_n, zl, (core + side) % 2),
+                sum_out.at[turn], sum_in.at[turn], e_send.at[turn], e_recv.at[turn], at_x(offsets[turn])
             )
             copy.start()
             e_copies.append(copy)
-    for copy in g_copies[x_n - 1]:
-        copy.wait_recv()
-    pair_out[...] = project(1 - core, x_n - 1)
-    pair_copy = remote(pair_out, pair_in, c_send, c_recv, other_core)
-    pair_copy.start()
-    total = project(core, x_n - 1) + bias
+    total = total + bias
     for turn in range(x_n - 1):
-        for side in range(2):
-            e_copies[2 * turn + side].wait_recv()
-            total = total + sum_in[turn, side].astype(F32)
-    pair_copy.wait_recv()
-    total = total + pair_in[...]
+        e_copies[turn].wait_recv()
+        total = total + sum_in[turn].astype(F32)
     out_ref[...] = total.astype(BF16)
-    for copies in (*s_copies, *wz_copies[1:], *z_copies, q_copies, r_copies, wp_copies, [pair_copy], e_copies):
+    for copies in (*s_copies, *z_copies, q_copies, r_copies, *wp_copies, c_copies, e_copies):
         for copy in copies:
             copy.wait_send()
 
-    @pl.when(jnp.logical_not(diagonal))
-    def _():
-        for copy in wz_copies[0]:
+    for when, copy in source_copies + tuple(relay_copies):
+
+        @pl.when(when)
+        def _():
             copy.wait_send()
 
     for sent in g_copies:
@@ -531,13 +577,13 @@
             pltpu.VMEM((2, zh_n, plane * GROUP // 2, LANES), BF16),
             pltpu.VMEM((2, zh_n, plane * GROUP // 2, LANES), BF16),
             pltpu.VMEM((x_n, y_n, share, LANES), BF16),
-            pltpu.VMEM((x_n, channels, LANES), BF16),
+            pltpu.VMEM((x_n, zl_n * x_share, LANES), BF16),
             pltpu.VMEM((zl_n, width, channels), BF16),
             pltpu.VMEM((zl_n, y_n, x_n, width, x_share), BF16),
-            pltpu.VMEM((outputs, LANES), F32),
-            pltpu.VMEM((outputs, LANES), F32),
-            pltpu.VMEM((x_n - 1, 2, outputs, LANES), BF16),
-            pltpu.VMEM((x_n - 1, 2, outputs, LANES), BF16),
+            pltpu.VMEM((x_n, outputs, LANES), F32),
+            pltpu.VMEM((x_n, outputs, LANES), F32),
+            pltpu.VMEM((x_n - 1, outputs, LANES), BF16),
+            pltpu.VMEM((x_n - 1, outputs, LANES), BF16),
             dma((11,)),
             dma((plane, 2)),
             dma((plane, 2)),
@@ -545,18 +591,19 @@
             dma((plane,)),
             dma((zh_n, 2)),
             dma((zh_n, 2)),
-            dma((zh_n, 2)),
+            dma((3,)),
             dma((zl_n, 2)),
-            dma((plane, 2)),
-            dma((plane, 2)),
+            dma((zl_n,)),
+            dma((zl_n, plane)),
+            dma((zl_n, plane)),
             dma((zh_n, 2)),
             dma((zh_n, 2)),
             dma((x_n, zl_n, y_n)),
             dma((x_n, zl_n, y_n)),
-            dma,
-            dma,
-            dma((x_n - 1, 2)),
-            dma((x_n - 1, 2)),
+            dma((x_n,)),
+            dma((x_n,)),
+            dma((x_n - 1,)),
+            dma((x_n - 1,)),
         ],
         compiler_params=pltpu.CompilerParams(
             collective_id=0, has_side_effects=True, vmem_limit_bytes=60 * 1024 * 1024

time: 83.4 us -> 75.3 us (0.903)
  the two profiles are of different devices: /device:TPU:33 before, /device:TPU:1 now
where the time goes in v4:
time: 75.3 us; the launch traced here: 75.1 us
  Pallas kernels  73.6 us (98%)
  local copies, waits for them, and re-layouts  1.57 us (2%)
    pallas_call x1, Pallas kernels, on_device(): pl.pallas_call(functools.partial(kernel, dims), out_shape=jax.ShapeDtypeS...  73.6 us
    unnamed x1, local copies, waits for them, and re-layouts  1.57 us

profile of v4, /device:TPU:1, one launch (start us, length us, event | category | flops | bytes accessed | tf_op | source)
XLA Modules:
  0.0 75.1 jit_solution(12423997889504976827)
XLA Ops:
  0.0 73.6 %hyena_mixer.1 = bf16[512,128]{1,0:T(8,128)(2,1)} custom-call(bf16[512,128]{1,0:T(8,128)(2,1)} %q_hbm.1, bf16[512,128]{1,0:T(8,128)(2,1)} %k_hbm.1, bf16[512,128]{1,0:T(8,128)(2,1)} %v_hbm.1, f32[512,128]{1,0:T(8,128)} %h_hbm.1, f32[1,512]{1,0:T(1,128)} %bitcast.4, bf16[64,512]{1,0:T(8,128)(2,1)} %bitcast.3, f32[1,512]{1,0:T(1,128)} %bitcast.5, ...), custom_call_target="tpu_custom_call" | custom-call | tf_op jit(solution)/shard_map/hyena_mixer/pallas_call | solution.py:556
  73.6 1.6 %copy.14 = bf16[512,128]{1,0:T(8,128)(2,1)} copy(bf16[512,128]{1,0:T(8,128)(2,1)} %hyena_mixer.1) | data formatting | bytes 262144

commit v5 on v4

--- a/solution.py
+++ b/solution.py
@@ -240,6 +240,27 @@
                 cut[part, y_at * x_n + x_at] = packed[start : start + zh_n // 2]
     pl.semaphore_wait(barrier, greeted + jnp.where(diagonal, 0, 2))
 
+    def own_piece(slot, step):
+        return remote(
+            w_hbm, w_line.at[zl], wz_send.at[slot], w_recv.at[zl], device((zh + step) % zh_n, y, x, zh)
+        )
+
+    source_copies = (
+        (zl >= zh, own_piece(0, 1)),
+        (zl <= zh, own_piece(1, last)),
+        (jnp.logical_not(diagonal), own_piece(2, 0)),
+    )
+    stay = pltpu.make_async_copy(w_hbm, w_line.at[zl], w_recv.at[zl])
+    for when, copy in source_copies:
+
+        @pl.when(when)
+        def _():
+            copy.start()
+
+    @pl.when(diagonal)
+    def _():
+        stay.start()
+
     s_copies = []
     for part in range(2):
         sent = []
@@ -254,38 +275,19 @@
             copy.start()
             sent.append(copy)
         s_copies.append(sent)
-    def own_piece(slot, step):
-        return remote(
-            w_hbm, w_line.at[zl], wz_send.at[slot], w_recv.at[zl], device((zh + step) % zh_n, y, x, zh)
-        )
-
-    source_copies = (
-        (zl >= zh, own_piece(0, 1)),
-        (zl <= zh, own_piece(1, last)),
-        (jnp.logical_not(diagonal), own_piece(2, 0)),
-    )
-    stay = pltpu.make_async_copy(w_hbm, w_line.at[zl], w_recv.at[zl])
-    for when, copy in source_copies:
-
-        @pl.when(when)
-        def _():
-            copy.start()
-
-    @pl.when(diagonal)
-    def _():
-        stay.start()
 
     def relay(part, step, slot, rows=slice(None)):
         piece = w_line.at[part, rows]
         return remote(piece, piece, wf_send.at[slot[0], slot[1]], w_recv.at[part], at_zh(step))
 
     relay_copies = []
+    inner_copies = []
     for part in range(zl_n):
         inner = jnp.logical_and(apart == 0, zl != part)
         for up in range(2):
             step = 1 if up else last
             side = (zl > part) if up else (zl < part)
-            relay_copies.append((jnp.logical_and(inner, side), relay(part, step, (part, up))))
+            inner_copies.append((jnp.logical_and(inner, side), relay(part, step, (part, up))))
         for up in range(2):
             step = 1 if up else last
             outer = apart == (1 if up else last)
@@ -296,6 +298,7 @@
                 (jnp.logical_and(outer, zl == part), relay(part, step, (part, up), rows))
             )
 
+    relay_copies += inner_copies
     wp_copies = []
     for part in range(zl_n):
         sent = []
@@ -328,6 +331,18 @@
     for load in loads[3:]:
         load.wait()
 
+    q_copies = []
+    for step in range(1, plane):
+        target = (place + step) % plane
+        rows = pl.ds(
+            pl.multiple_of(target % x_n * x_share + target // x_n * share, share), share
+        )
+        copy = remote(
+            q_hbm.at[rows], query_in.at[place], q_send.at[step], q_recv.at[step], in_plane(step)
+        )
+        copy.start()
+        q_copies.append(copy)
+
     index = lax.broadcasted_iota(jnp.int32, (share, 1), 0)
     skip = column(skip_ref[...], x * x_share + y * share + index).reshape(zh_n, 1, GROUP, 1)
     z_copies = []
@@ -357,18 +372,6 @@
     for zh_at in range(zh_n):
         first, second = (value[zh_at // 2, :, zh_at % 2] for value in arrived)
         direct[:, zh_at] = skip[zh_at] * low_high(first, second, False, True)
-    q_copies = []
-    for step in range(1, plane):
-        target = (place + step) % plane
-        rows = pl.ds(
-            pl.multiple_of(target % x_n * x_share + target // x_n * share, share), share
-        )
-        copy = remote(
-            q_hbm.at[rows], query_in.at[place], q_send.at[step], q_recv.at[step], in_plane(step)
-        )
-        copy.start()
-        q_copies.append(copy)
-
     for part in range(zl_n):
 
         @pl.when(direct_piece(part))

time: 75.3 us -> 74.7 us (level)
  no operation moved by 1% of the time
where the time goes in v5:
time: 74.7 us; the launch traced here: 74.5 us
  Pallas kernels  72.9 us (98%)
  local copies, waits for them, and re-layouts  1.57 us (2%)
    pallas_call x1, Pallas kernels, on_device(): pl.pallas_call(functools.partial(kernel, dims), out_shape=jax.ShapeDtypeS...  72.9 us
    unnamed x1, local copies, waits for them, and re-layouts  1.57 us

profile of v5, /device:TPU:1, one launch (start us, length us, event | category | flops | bytes accessed | tf_op | source)
XLA Modules:
  0.0 74.5 jit_solution(11850371434142937443)
XLA Ops:
  0.0 72.9 %hyena_mixer.1 = bf16[512,128]{1,0:T(8,128)(2,1)} custom-call(bf16[512,128]{1,0:T(8,128)(2,1)} %q_hbm.1, bf16[512,128]{1,0:T(8,128)(2,1)} %k_hbm.1, bf16[512,128]{1,0:T(8,128)(2,1)} %v_hbm.1, f32[512,128]{1,0:T(8,128)} %h_hbm.1, f32[1,512]{1,0:T(1,128)} %bitcast.4, bf16[64,512]{1,0:T(8,128)(2,1)} %bitcast.3, f32[1,512]{1,0:T(1,128)} %bitcast.5, ...), custom_call_target="tpu_custom_call" | custom-call | tf_op jit(solution)/shard_map/hyena_mixer/pallas_call | solution.py:559
  73.0 1.6 %copy.14 = bf16[512,128]{1,0:T(8,128)(2,1)} copy(bf16[512,128]{1,0:T(8,128)(2,1)} %hyena_mixer.1) | data formatting | bytes 262144
